TPU v7x, 256 devices: a whole 4x4x8 slice. The times are simulated.
256 devices in a mesh: dp: 256 (over x, z, y, core).
Axes of the slice: x: 4, y: 4, z: 8, core: 2. Of those that a mesh axis runs over, the one named last changes fastest.
Arguments:
- image_features: bfloat16 [32768, 1152], P('dp'), may hold values from -0.59765625 to 0.59765625
- text_features: bfloat16 [32768, 1152], P('dp'), may hold values from -0.59765625 to 0.59765625
- projections: bfloat16 [2304, 1152], P('dp'), may hold values from -0.1875 to 0.1875
- labels: int32 [32768], P('dp'), may hold values from 0 to 32767, as said below
Outputs:
- image_grad: float32 [32768, 1152], P('dp')
- text_grad: float32 [32768, 1152], P('dp')
Inputs may be any that keep to these rules, and one draw needn't show every extreme that they name: For each block k of 128 rows, the labels are the 128 text rows of one block (k - s) mod 256, each once, with s between 0 and 31 drawn for each block.
All inputs are finite; a program needn't handle non-finite values.
Results may differ from a plain program's by a relative error of at most 0.01.
Values may be sent and summed in bfloat16 or wider, within the bound.
No kernel may reach another device: no remote copies, remote signals or barrier semaphores. Data moves between devices by JAX's collectives and lax.ppermute only.
A program may use at most 128 MiB of HBM per device.

v0:
```python
import jax
import jax.numpy as jnp
from jax import lax
from jax.experimental import pallas as pl
from jax.experimental.pallas import tpu as pltpu
from jax.sharding import Mesh, PartitionSpec as P

AXES = ("x", "z", "y", "c")
SIZES = (4, 8, 4, 2)
WINDOW_PLANES = 4

logit_scale = 10.0
logit_bias = -2.0
eps = 1e-06
contract_last = (((1,), (1,)), ((), ()))
contract_first = (((0,), (0,)), ((), ()))


def along(value, axis, steps):
    count = lax.axis_size(axis)
    return lax.ppermute(value, axis, [(i, (i + steps) % count) for i in range(count)])


def blocks_behind(value, steps):
    return lax.ppermute(value, AXES, [(i, (i + steps) % 256) for i in range(256)])


def device(x, z, y, c):
    return ((x * 8 + z) * 4 + y) * 2 + c


def everyone():
    return [(x, z, y, c) for x in range(4) for z in range(8) for y in range(4) for c in range(2)]


def crosswise(value, core0_axis, steps):
    pairs = []
    for x, z, y, c in everyone():
        if (core0_axis == "x") == (c == 0):
            source = device((x + steps) % 4, z, y, c)
        else:
            source = device(x, z, (y + steps) % 4, c)
        pairs.append((source, device(x, z, y, c)))
    return lax.ppermute(value, AXES, pairs)


def order_shards(where_ref, *refs):
    chips, out_ref, wide_ref = refs[:4], refs[4], refs[5]
    height = chips[0].shape[0] // 2
    for n in range(8):
        slot = 2 * lax.rem(where_ref[0] + n // 2, 4) + lax.rem(where_ref[1] + n % 2, 2)
        shard = chips[n // 2][...].astype(jnp.float32)
        for row in range(height):
            at = n % 2 * height + row
            wide_ref[pl.ds(slot * height + row, 1), :] = shard[at : at + 1]
    out_ref[...] = wide_ref[...].astype(out_ref.dtype)


def order_units(where_ref, *refs):
    units, out_ref, wide_ref = refs[:4], refs[4], refs[5]
    height = units[0].shape[0]
    for n, unit_ref in enumerate(units):
        at = pl.multiple_of(lax.rem(where_ref[0] + n, 4) * height, 8)
        wide_ref[pl.ds(at, height), :] = unit_ref[...].astype(jnp.float32)
    out_ref[...] = wide_ref[...].astype(out_ref.dtype)


def on_device(body, where, arrays, outs, scratch=(), flops=0, vmem=8, anywhere=0):
    out_bytes = sum(o.size * o.dtype.itemsize for o in outs) + sum(v.size * v.dtype.itemsize for v in arrays)
    return pl.pallas_call(
        body,
        out_shape=outs,
        in_specs=[pl.BlockSpec(memory_space=pltpu.SMEM)]
        + [pl.BlockSpec(memory_space=pl.ANY)] * anywhere
        + [pl.BlockSpec(memory_space=pltpu.VMEM)] * (len(arrays) - anywhere),
        out_specs=[pl.BlockSpec(memory_space=pltpu.VMEM)] * len(outs),
        scratch_shapes=list(scratch),
        compiler_params=pltpu.CompilerParams(vmem_limit_bytes=vmem << 20),
        cost_estimate=pl.CostEstimate(flops=flops, bytes_accessed=out_bytes, transcendentals=0),
    )(jnp.stack(where).astype(jnp.int32), *arrays)


def like(rows, width, dtype):
    return jax.ShapeDtypeStruct((rows, width), dtype)


def unit_place(x, z, y, c):
    high, low = (x % 2) * 2 + z // 4, z % 4
    tx, ty = ((high + 3) % 4, low) if x < 2 else (low, high)
    far = [z, z + 1, z - 1, z + 2, z - 2, z + 3, z - 3, z + 4]
    rank = 2 * {0: 3, 1: 1, 3: 2, 2: 0}[(y - ty) % 4] + c
    return (tx, far[rank] % 8, ty, x // 2)


def start_weights(shard):
    y, c = lax.axis_index("y"), lax.axis_index("c")
    chip = jnp.concatenate([shard, along(shard, "c", 1)])
    chips = [chip, along(chip, "y", -1), along(chip, "y", 2), along(chip, "y", 1)]
    height, width = 4 * chip.shape[0], chip.shape[1]
    (unit,) = on_device(
        order_shards, (y, c), chips, [like(height, width, shard.dtype)], [pltpu.VMEM((height, width), jnp.float32)]
    )
    return unit


def spread_units(unit):
    pairs = [(device(*source), device(*unit_place(*source))) for source in everyone()]
    return lax.ppermute(unit, AXES, pairs)


def gather_near(unit):
    return [unit] + [crosswise(unit, "y", d) for d in (1, 2, 3)]


def join_units(near):
    x, y, c = lax.axis_index("x"), lax.axis_index("y"), lax.axis_index("c")
    height, width = 4 * near[0].shape[0], near[0].shape[1]
    (block,) = on_device(
        order_units, (jnp.where(c == 0, y, x),), near, [like(height, width, near[0].dtype)],
        [pltpu.VMEM((height, width), jnp.float32)],
    )
    return block


def place(where_ref, on_core0, pieces, weight, sems):
    for core_is_0 in (True, False):

        @pl.when((where_ref[0] == 0) if core_is_0 else (where_ref[0] != 0))
        def _():
            own = core_is_0 == on_core0
            block = pieces[0].shape[0]
            first = where_ref[1] if own else where_ref[2]
            copies = []
            for n in range(4):
                at = pl.multiple_of(lax.rem(first + n, 4) * block, 32)
                piece = pieces[n if own else 4 + n]
                copies.append(pltpu.make_async_copy(piece, weight.at[pl.ds(at, block)], sems.at[n]))
            for copy in copies:
                copy.start()
            for copy in copies:
                copy.wait()


def embed(sources, weight, emb, unit_ref, norm_ref):
    rows, width = unit_ref.shape
    for first in range(0, len(sources), 2):
        some = sources[first : first + 2]
        features = jnp.concatenate([source[:, :width] for source in some])
        unit, norm = normalize(jnp.dot(features, weight[...], preferred_element_type=jnp.float32))
        emb[pl.ds(first * rows, len(some) * rows), :width] = unit.astype(jnp.bfloat16)
        if first == 0:
            unit_ref[...] = unit[:rows]
            norm_ref[...] = jnp.broadcast_to(norm[:rows], norm_ref.shape)


def embed_images(where_ref, *refs):
    weight, emb, unit_ref, norm_ref, sems = refs[12:]
    place(where_ref, True, refs[:8], weight, sems)
    images = refs[8:12]
    embed(images, weight, emb, unit_ref, norm_ref)
    rows, width = unit_ref.shape
    for slot, image in enumerate(images):
        emb[slot * rows : (slot + 1) * rows, width:] = image[:, width:]


def embed_texts(where_ref, *refs):
    weight, emb, unit_ref, norm_ref, sems = refs[13:]
    place(where_ref, False, refs[:8], weight, sems)
    embed(refs[8:13], weight, emb, unit_ref, norm_ref)


def text_sum(own_coeff, other_coeff, own_emb, other_emb, plane):
    width = own_emb.shape[1] - 128
    rows = own_emb.shape[0] // 4
    total = 0.0
    for coeff, emb in ((own_coeff, own_emb), (other_coeff, other_emb)):
        total = total + lax.dot_general(
            coeff[:, plane * rows : (plane + 1) * rows], emb[:, :width], contract_first,
            preferred_element_type=jnp.float32,
        )
    return total


def weigh_pairs(where_ref, own_emb, other_emb, text_emb, own_coeff, other_coeff, far_ref):
    core, y = where_ref[0], where_ref[3]
    rows, width = text_emb.shape[0] // 5, text_emb.shape[1]
    column = lax.broadcasted_iota(jnp.int32, (rows, rows), 1)
    for kind, (emb, coeff_ref) in enumerate(((own_emb, own_coeff), (other_emb, other_coeff))):
        for first in (0, 2):
            logits = logit_bias + logit_scale * lax.dot_general(
                emb[first * rows : (first + 2) * rows, :width], text_emb[...], contract_last,
                preferred_element_type=jnp.float32,
            )
            chance = jax.nn.sigmoid(logits)
            for slot in (first, first + 1):
                ahead = 2 * lax.rem(y + slot, 4) + lax.rem(core + kind, 2)
                at = slice(slot * rows, (slot + 1) * rows)
                marks = emb[at, width:].astype(jnp.float32).astype(jnp.int32)
                behind, label = marks[:, 0:1], marks[:, 1:2]
                hit = column == label
                for plane in range(WINDOW_PLANES + 1):
                    distance = ahead + 8 * plane - (2 * y + core)
                    columns = slice(plane * rows, (plane + 1) * rows)
                    tile = chance[(slot - first) * rows : (slot - first + 1) * rows, columns]
                    tile = tile - jnp.where(hit & (behind == distance), 1.0, 0.0)
                    if plane in (0, WINDOW_PLANES):
                        tile = tile * jnp.where((distance >= 0) & (distance < 8 * WINDOW_PLANES), 1.0, 0.0)
                    coeff_ref[at, columns] = tile.astype(jnp.bfloat16)
    far_ref[...] = text_sum(own_coeff, other_coeff, own_emb, other_emb, WINDOW_PLANES).astype(far_ref.dtype)


def sum_pairs(where_ref, own_coeff, other_coeff, own_emb, other_emb, text_emb, *outs):
    rows = own_emb.shape[0] // 4
    text_sums, kept, sent = outs[:4], outs[4:8], outs[8:]
    for plane in range(WINDOW_PLANES):
        text_sums[plane][...] = text_sum(own_coeff, other_coeff, own_emb, other_emb, plane)
    for first in (0, 2):
        at = slice(first * rows, (first + 2) * rows)
        both = jnp.dot(own_coeff[at, :], text_emb[...], preferred_element_type=jnp.float32)
        kept[first][...] = both[:rows]
        kept[first + 1][...] = both[rows:]
        both = jnp.dot(other_coeff[at, :], text_emb[...], preferred_element_type=jnp.float32)
        sent[first][...] = both[:rows].astype(jnp.bfloat16)
        sent[first + 1][...] = both[rows:].astype(jnp.bfloat16)


def finish(where_ref, sum_ref, unit_ref, norm_ref, weight_ref, *refs):
    arrived, grad_ref = refs[:-1], refs[-1]
    total = sum_ref[...]
    for one in arrived:
        total = total + one[...].astype(jnp.float32)
    draw = unproject(unit_ref[...], norm_ref[:, 0:1], logit_scale * total)
    grad_ref[...] = lax.dot_general(draw, weight_ref[...], contract_last, preferred_element_type=jnp.float32)


def normalize(raw):
    norm = jnp.sqrt(jnp.sum(raw * raw, axis=-1, keepdims=True) + eps)
    return (raw * (1.0 / norm), norm)


def unproject(unit, norm, grad):
    inner = jnp.sum(unit * grad, axis=-1, keepdims=True)
    return ((grad - unit * inner) * (1.0 / norm)).astype(jnp.bfloat16)


def per_device(image_features, text_features, projections, labels):
    rows, width = image_features.shape
    x, z, y, c = (lax.axis_index(a) for a in AXES)
    index = lax.axis_index(AXES)
    tied = lax.optimization_barrier

    marks = jnp.stack([(index - labels // rows) % 256, labels % rows], axis=1).astype(image_features.dtype)
    marked = jnp.concatenate([image_features, jnp.pad(marks, ((0, 0), (0, 126)))], axis=1)

    hop1 = blocks_behind(text_features, 8)
    unit, hop1, marked = tied((start_weights(projections), hop1, marked))
    hop2 = blocks_behind(hop1, 8)
    around = [along(marked, "y", -1), along(marked, "y", 2), along(marked, "y", 1)]
    unit, hop2, *around = tied((spread_units(unit), hop2, *around))
    hop3 = blocks_behind(hop2, 8)
    hop3, *near = tied((hop3, *gather_near(unit)))
    block = join_units(near)
    hop4 = blocks_behind(hop3, 8)
    pieces = [block] + [crosswise(block, "x", d) for d in (1, 2, 3)]
    swapped = along(block, "c", 1)
    hop4, swapped, *pieces = tied((hop4, swapped, *pieces))
    pieces = pieces + [swapped] + [along(piece, "c", 1) for piece in pieces[1:]]
    images, texts = [marked, *around], [text_features, hop1, hop2, hop3, hop4]

    whole = like(4 * block.shape[0], width, block.dtype)
    first_x, first_y = (x + 1) % 4, y
    where = (c, jnp.where(c == 0, first_x, first_y), jnp.where(c == 0, first_y, first_x), y)
    wide, narrow = like(rows, width, jnp.float32), like(rows, 128, jnp.float32)
    low = jnp.bfloat16
    sems = [pltpu.SemaphoreType.DMA((4,))]
    image_weight, image_emb, image_unit, image_norm = on_device(
        embed_images, where, pieces + images, [whole, like(4 * rows, width + 128, low), wide, narrow], sems,
        flops=8 * rows * width * width, vmem=16, anywhere=8,
    )
    other_emb = along(image_emb, "c", 1)
    text_weight, text_emb, text_unit, text_norm = on_device(
        embed_texts, where, pieces + texts, [whole, like(5 * rows, width, low), wide, narrow], sems,
        flops=10 * rows * width * width, vmem=16, anywhere=8,
    )
    coeff, other_coeff, far = on_device(
        weigh_pairs, where, [image_emb, other_emb, text_emb],
        [like(4 * rows, 5 * rows, low), like(4 * rows, 5 * rows, low), like(rows, width, low)],
        flops=96 * rows * rows * width, vmem=20,
    )
    far = blocks_behind(far, -8)
    sums = on_device(
        sum_pairs, (y,), [coeff, other_coeff, image_emb, other_emb, text_emb],
        [wide] * 8 + [like(rows, width, low)] * 4,
        flops=2 * 72 * rows * rows * width, vmem=20,
    )
    text_sums, kept, sent = sums[:4], sums[4:8], sums[8:]

    far = blocks_behind((far.astype(jnp.float32) + text_sums[3]).astype(low), -8)
    chip = [kept[dy] + along(sent[dy], "c", 1).astype(jnp.float32) for dy in range(4)]
    arrived = [along(chip[dy].astype(low), "y", steps) for dy, steps in ((1, 1), (2, 2), (3, -1))]
    far, arrived[0] = tied((far, arrived[0]))
    far = blocks_behind((far.astype(jnp.float32) + text_sums[2]).astype(low), -8)
    far, arrived[2] = tied((far, arrived[2]))
    far = blocks_behind((far.astype(jnp.float32) + text_sums[1]).astype(low), -8)
    flops = 2 * rows * width * width
    (image_grad,) = on_device(finish, (y,), [chip[0], image_unit, image_norm, image_weight, *arrived], [wide], flops=flops, vmem=16)
    (text_grad,) = on_device(finish, (y,), [text_sums[0], text_unit, text_norm, text_weight, far], [wide], flops=flops, vmem=16)
    return (image_grad, text_grad)


def solution(mesh):
    fine = Mesh(mesh.devices.reshape(SIZES), AXES)
    rows = P(AXES, None)
    return jax.shard_map(
        per_device,
        mesh=fine,
        in_specs=(rows, rows, rows, P(AXES)),
        out_specs=(rows, rows),
        check_vma=False,
    )
```

profile of v0, /device:TPU:0, one launch (start us, length us, event | category | flops | bytes accessed | tf_op | source)
XLA Modules:
  0.0 136.3 jit_solution(7714880680982754888)
XLA Ops:
  3.7 1.7 %collective-permute-start.3 = (bf16[18,1152]{1,0:T(8,128)(2,1)S(1)}, bf16[18,1152]{1,0:T(8,128)(2,1)S(1)}, u32[]{:S(2)}, u32[]{:S(2)}) collective-permute-start(bf16[18,1152]{1,0:T(8,128)(2,1)S(1)} %pad_maximum_fusion.refs_0_), channel_id=1, source_target_pairs={{0,2},{2,4},{4,6},{6,0},{1,3},{3,5},{5,7},{7,1},{8,10},{10,12},{12... | collective-permute-start | bytes 124424 | tf_op jit(solution)/shard_map/ppermute | solution.py:21
  5.3 2.9 %collective-permute-start.2 = (bf16[18,1152]{1,0:T(8,128)(2,1)S(1)}, bf16[18,1152]{1,0:T(8,128)(2,1)S(1)}, u32[]{:S(2)}, u32[]{:S(2)}) collective-permute-start(bf16[18,1152]{1,0:T(8,128)(2,1)S(1)} %pad_maximum_fusion.refs_0_), channel_id=1, source_target_pairs={{0,4},{2,6},{4,0},{6,2},{1,5},{3,7},{5,1},{7,3},{8,12},{10,14},{12... | collective-permute-start | bytes 124424 | tf_op jit(solution)/shard_map/ppermute | solution.py:21
  9.7 1.7 %collective-permute-done.2.refs_2_ = bf16[18,1152]{1,0:T(8,128)(2,1)S(1)} collective-permute-done((bf16[18,1152]{1,0:T(8,128)(2,1)S(1)}, bf16[18,1152]{1,0:T(8,128)(2,1)S(1)}, u32[]{:S(2)}, u32[]{:S(2)}) %collective-permute-start.2) | collective-permute-done | bytes 41504 | tf_op jit(solution)/shard_map/ppermute | solution.py:21
  13.1 1.8 %collective-permute-done.4.refs_9_ = bf16[128,1152]{1,0:T(8,128)(2,1)S(1)} collective-permute-done((bf16[128,1152]{1,0:T(8,128)(2,1)}, bf16[128,1152]{1,0:T(8,128)(2,1)S(1)}, u32[]{:S(2)}, u32[]{:S(2)}) %collective-permute-start.4) | collective-permute-done | bytes 294944 | tf_op jit(solution)/shard_map/ppermute | solution.py:25
  14.9 1.6 %collective-permute-start.9 = (bf16[128,1280]{1,0:T(8,128)(2,1)S(1)}, bf16[128,1280]{1,0:T(8,128)(2,1)S(1)}, u32[]{:S(2)}, u32[]{:S(2)}) collective-permute-start(bf16[128,1280]{1,0:T(8,128)(2,1)S(1)} %fusion.1.refs_8_), channel_id=1, source_target_pairs={{0,2},{2,4},{4,6},{6,0},{1,3},{3,5},{5,7},{7,1},{8,10},{10,12},{12... | collective-permute-start | bytes 983048 | tf_op jit(solution)/shard_map/ppermute | solution.py:21
  16.5 2.9 %collective-permute-start.8 = (bf16[128,1280]{1,0:T(8,128)(2,1)S(1)}, bf16[128,1280]{1,0:T(8,128)(2,1)S(1)}, u32[]{:S(2)}, u32[]{:S(2)}) collective-permute-start(bf16[128,1280]{1,0:T(8,128)(2,1)S(1)} %fusion.1.refs_8_), channel_id=1, source_target_pairs={{0,4},{2,6},{4,0},{6,2},{1,5},{3,7},{5,1},{7,3},{8,12},{10,14},{12... | collective-permute-start | bytes 983048 | tf_op jit(solution)/shard_map/ppermute | solution.py:21
  21.5 5.6 %collective-permute-start.5 = (bf16[72,1152]{1,0:T(8,128)(2,1)S(1)}, bf16[72,1152]{1,0:T(8,128)(2,1)S(1)}, u32[]{:S(2)}, u32[]{:S(2)}) collective-permute-start(bf16[72,1152]{1,0:T(8,128)(2,1)S(1)} %shard_map.59), channel_id=1, source_target_pairs={{0,232},{1,224},{2,248},{3,208},{4,192},{5,200},{6,240},{7,216},{8... | collective-permute-start | bytes 497672 | tf_op jit(solution)/shard_map/ppermute | solution.py:108
  27.1 4.7 %collective-permute-done.5.refs_0_ = bf16[72,1152]{1,0:T(8,128)(2,1)S(1)} collective-permute-done((bf16[72,1152]{1,0:T(8,128)(2,1)S(1)}, bf16[72,1152]{1,0:T(8,128)(2,1)S(1)}, u32[]{:S(2)}, u32[]{:S(2)}) %collective-permute-start.5) | collective-permute-done | bytes 165920 | tf_op jit(solution)/shard_map/ppermute | solution.py:108
  31.8 3.8 %collective-permute-done.6.refs_10_ = bf16[128,1152]{1,0:T(8,128)(2,1)S(1)} collective-permute-done((bf16[128,1152]{1,0:T(8,128)(2,1)S(1)}, bf16[128,1152]{1,0:T(8,128)(2,1)S(1)}, u32[]{:S(2)}, u32[]{:S(2)}) %collective-permute-start.6) | collective-permute-done | bytes 294944 | tf_op jit(solution)/shard_map/ppermute | solution.py:25
  38.5 3.7 %collective-permute-start.12 = (bf16[72,1152]{1,0:T(8,128)(2,1)S(1)}, bf16[72,1152]{1,0:T(8,128)(2,1)S(1)}, u32[]{:S(2)}, u32[]{:S(2)}) collective-permute-start(bf16[72,1152]{1,0:T(8,128)(2,1)S(1)} %collective-permute-done.5.refs_0_), channel_id=1, source_target_pairs={{4,0},{129,1},{6,2},{131,3},{0,4},{133,5},{2,6},{135,7},{12,8},{13... | collective-permute-start | bytes 497672 | tf_op jit(solution)/shard_map/ppermute | solution.py:44
  43.3 1.7 %collective-permute-done.13.refs_3_ = bf16[72,1152]{1,0:T(8,128)(2,1)S(1)} collective-permute-done((bf16[72,1152]{1,0:T(8,128)(2,1)S(1)}, bf16[72,1152]{1,0:T(8,128)(2,1)S(1)}, u32[]{:S(2)}, u32[]{:S(2)}) %collective-permute-start.13) | collective-permute-done | bytes 165920 | tf_op jit(solution)/shard_map/ppermute | solution.py:44
  45.0 2.2 %collective-permute-done.12.refs_2_ = bf16[72,1152]{1,0:T(8,128)(2,1)S(1)} collective-permute-done((bf16[72,1152]{1,0:T(8,128)(2,1)S(1)}, bf16[72,1152]{1,0:T(8,128)(2,1)S(1)}, u32[]{:S(2)}, u32[]{:S(2)}) %collective-permute-start.12) | collective-permute-done | bytes 165920 | tf_op jit(solution)/shard_map/ppermute | solution.py:44
  49.5 1.9 %collective-permute-start.18 = (bf16[288,1152]{1,0:T(8,128)(2,1)S(1)}, bf16[288,1152]{1,0:T(8,128)(2,1)S(1)}, u32[]{:S(2)}, u32[]{:S(2)}) collective-permute-start(bf16[288,1152]{1,0:T(8,128)(2,1)S(1)} %shard_map.60.refs_0_), channel_id=1, source_target_pairs={{192,0},{7,1},{194,2},{1,3},{196,4},{3,5},{198,6},{5,7},{200,8},{1... | collective-permute-start | bytes 1990664 | tf_op jit(solution)/shard_map/ppermute | solution.py:44
  54.2 1.9 %collective-permute-start.15 = (bf16[288,1152]{1,0:T(8,128)(2,1)S(1)}, bf16[288,1152]{1,0:T(8,128)(2,1)S(1)}, u32[]{:S(2)}, u32[]{:S(2)}) collective-permute-start(bf16[288,1152]{1,0:T(8,128)(2,1)S(1)} %shard_map.60.refs_0_), channel_id=1, source_target_pairs={{0,1},{1,0},{2,3},{3,2},{4,5},{5,4},{6,7},{7,6},{8,9},{9,8},{10,11... | collective-permute-start | bytes 1990664 | tf_op jit(solution)/shard_map/ppermute | solution.py:21
  56.2 13.0 %collective-permute-done.14.refs_12_ = bf16[128,1152]{1,0:T(8,128)(2,1)S(1)} collective-permute-done((bf16[128,1152]{1,0:T(8,128)(2,1)}, bf16[128,1152]{1,0:T(8,128)(2,1)S(1)}, u32[]{:S(2)}, u32[]{:S(2)}) %collective-permute-start.14) | collective-permute-done | bytes 294944 | tf_op jit(solution)/shard_map/ppermute | solution.py:25
  69.9 5.7 %collective-permute-done.17.refs_2_ = bf16[288,1152]{1,0:T(8,128)(2,1)S(1)} collective-permute-done((bf16[288,1152]{1,0:T(8,128)(2,1)S(1)}, bf16[288,1152]{1,0:T(8,128)(2,1)S(1)}, u32[]{:S(2)}, u32[]{:S(2)}) %collective-permute-start.17) | collective-permute-done | bytes 663584 | tf_op jit(solution)/shard_map/ppermute | solution.py:44
  83.7 3.6 %shard_map.61 = (bf16[1152,1152]{1,0:T(8,128)(2,1)S(1)}, bf16[512,1280]{1,0:T(8,128)(2,1)S(1)}, f32[128,1152]{1,0:T(8,128)S(1)}, f32[128,128]{1,0:T(8,128)S(1)}) custom-call(s32[4]{0:T(128)S(1)} %pad_add_fusion.where_ref, bf16[288,1152]{1,0:T(8,128)(2,1)S(1)} %shard_map.60.refs_0_, bf16[288,1152]{1,0:T(8,128)(2,1)S(1)} %collective-permute-done.16.refs_1_, ...), custom_call_target="tpu_custom_call" | custom-call | flops 1358954496 | bytes 11239424 | tf_op jit(solution)/shard_map/pallas_call | solution.py:70
  88.3 4.8 %shard_map.62 = (bf16[1152,1152]{1,0:T(8,128)(2,1)S(1)}, bf16[640,1152]{1,0:T(8,128)(2,1)S(1)}, f32[128,1152]{1,0:T(8,128)S(1)}, f32[128,128]{1,0:T(8,128)S(1)}) custom-call(s32[4]{0:T(128)S(1)} %pad_add_fusion.where_ref, bf16[288,1152]{1,0:T(8,128)(2,1)S(1)} %shard_map.60.refs_0_, bf16[288,1152]{1,0:T(8,128)(2,1)S(1)} %collective-permute-done.16.refs_1_, ...), custom_call_target="tpu_custom_call" | custom-call | flops 1698693120 | bytes 11567104 | tf_op jit(solution)/shard_map/pallas_call | solution.py:70
  93.2 3.6 %shard_map.63 = (bf16[512,640]{1,0:T(8,128)(2,1)S(1)}, bf16[512,640]{1,0:T(8,128)(2,1)S(1)}, bf16[128,1152]{1,0:T(8,128)(2,1)S(1)}) custom-call(s32[4]{0:T(128)S(1)} %pad_add_fusion.where_ref, bf16[512,1280]{1,0:T(8,128)(2,1)S(1)} %get-tuple-element.66.own_emb, bf16[512,1280]{1,0:T(8,128)(2,1)S(1)} %collective-permute-done.22.other_emb, ...), custom_call_target="tpu_custom_call" | custom-call | flops 1811939328 | bytes 5701632 | tf_op jit(solution)/shard_map/pallas_call | solution.py:70
  97.1 3.6 %shard_map.64 = (f32[128,1152]{1,0:T(8,128)S(1)}, f32[128,1152]{1,0:T(8,128)S(1)}, f32[128,1152]{1,0:T(8,128)S(1)}, f32[128,1152]{1,0:T(8,128)S(1)}, f32[128,115...) custom-call(s32[1]{0:T(128)} %bitcast.where_ref, ...), custom_call_target="tpu_custom_call" | custom-call | flops 2717908992 | bytes 11304960 | tf_op jit(solution)/shard_map/pallas_call | solution.py:70
  101.8 3.5 %collective-permute-done.24 = bf16[128,1152]{1,0:T(8,128)(2,1)S(1)} collective-permute-done((bf16[128,1152]{1,0:T(8,128)(2,1)S(1)}, bf16[128,1152]{1,0:T(8,128)(2,1)S(1)}, u32[]{:S(2)}, u32[]{:S(2)}) %collective-permute-start.24) | collective-permute-done | bytes 294944 | tf_op jit(solution)/shard_map/ppermute | solution.py:25
  105.3 3.7 %collective-permute-start.25 = (bf16[128,1152]{1,0:T(8,128)(2,1)S(1)}, bf16[128,1152]{1,0:T(8,128)(2,1)S(1)}, u32[]{:S(2)}, u32[]{:S(2)}) collective-permute-start(bf16[128,1152]{1,0:T(8,128)(2,1)S(1)} %add_convert_fusion.5), channel_id=1, source_target_pairs={{0,248},{1,249},{2,250},{3,251},{4,252},{5,253},{6,254},{7,255},{8... | collective-permute-start | bytes 884744 | tf_op jit(solution)/shard_map/ppermute | solution.py:25
  109.1 1.8 %collective-permute-start.27 = (bf16[128,1152]{1,0:T(8,128)(2,1)S(1)}, bf16[128,1152]{1,0:T(8,128)(2,1)S(1)}, u32[]{:S(2)}, u32[]{:S(2)}) collective-permute-start(bf16[128,1152]{1,0:T(8,128)(2,1)S(1)} %add_convert_fusion.4), channel_id=1, source_target_pairs={{0,2},{2,4},{4,6},{6,0},{1,3},{3,5},{5,7},{7,1},{8,10},{10,12},{12... | collective-permute-start | bytes 884744 | tf_op jit(solution)/shard_map/ppermute | solution.py:21
  111.0 1.6 %collective-permute-start.32 = (bf16[128,1152]{1,0:T(8,128)(2,1)S(1)}, bf16[128,1152]{1,0:T(8,128)(2,1)S(1)}, u32[]{:S(2)}, u32[]{:S(2)}) collective-permute-start(bf16[128,1152]{1,0:T(8,128)(2,1)S(1)} %add_convert_fusion.1), channel_id=1, source_target_pairs={{0,6},{2,0},{4,2},{6,4},{1,7},{3,1},{5,3},{7,5},{8,14},{10,8},{12,... | collective-permute-start | bytes 884744 | tf_op jit(solution)/shard_map/ppermute | solution.py:21
  114.1 3.6 %collective-permute-done.27.refs_0_ = bf16[128,1152]{1,0:T(8,128)(2,1)S(1)} collective-permute-done((bf16[128,1152]{1,0:T(8,128)(2,1)S(1)}, bf16[128,1152]{1,0:T(8,128)(2,1)S(1)}, u32[]{:S(2)}, u32[]{:S(2)}) %collective-permute-start.27) | collective-permute-done | bytes 294944 | tf_op jit(solution)/shard_map/ppermute | solution.py:21
  117.7 2.3 %collective-permute-start.30 = (bf16[128,1152]{1,0:T(8,128)(2,1)S(1)}, bf16[128,1152]{1,0:T(8,128)(2,1)S(1)}, u32[]{:S(2)}, u32[]{:S(2)}) collective-permute-start(bf16[128,1152]{1,0:T(8,128)(2,1)S(1)} %add_convert_fusion.2), channel_id=1, source_target_pairs={{0,248},{1,249},{2,250},{3,251},{4,252},{5,253},{6,254},{7,255},{8... | collective-permute-start | bytes 884744 | tf_op jit(solution)/shard_map/ppermute | solution.py:25
  120.1 1.6 %collective-permute-start.29 = (bf16[128,1152]{1,0:T(8,128)(2,1)S(1)}, bf16[128,1152]{1,0:T(8,128)(2,1)S(1)}, u32[]{:S(2)}, u32[]{:S(2)}) collective-permute-start(bf16[128,1152]{1,0:T(8,128)(2,1)S(1)} %add_convert_fusion.3), channel_id=1, source_target_pairs={{0,4},{2,6},{4,0},{6,2},{1,5},{3,7},{5,1},{7,3},{8,12},{10,14},{12... | collective-permute-start | bytes 884744 | tf_op jit(solution)/shard_map/ppermute | solution.py:21
  121.7 3.4 %collective-permute-done.30 = bf16[128,1152]{1,0:T(8,128)(2,1)S(1)} collective-permute-done((bf16[128,1152]{1,0:T(8,128)(2,1)S(1)}, bf16[128,1152]{1,0:T(8,128)(2,1)S(1)}, u32[]{:S(2)}, u32[]{:S(2)}) %collective-permute-start.30) | collective-permute-done | bytes 294944 | tf_op jit(solution)/shard_map/ppermute | solution.py:25
  125.1 5.0 %collective-permute-start.33 = (bf16[128,1152]{1,0:T(8,128)(2,1)S(1)}, bf16[128,1152]{1,0:T(8,128)(2,1)S(1)}, u32[]{:S(2)}, u32[]{:S(2)}) collective-permute-start(bf16[128,1152]{1,0:T(8,128)(2,1)S(1)} %add_convert_fusion), channel_id=1, source_target_pairs={{0,248},{1,249},{2,250},{3,251},{4,252},{5,253},{6,254},{7,255},{8... | collective-permute-start | bytes 884744 | tf_op jit(solution)/shard_map/ppermute | solution.py:25
  130.3 1.9 %shard_map.65 = f32[128,1152]{1,0:T(8,128)} custom-call(s32[1]{0:T(128)} %bitcast.where_ref, f32[128,1152]{1,0:T(8,128)S(1)} %convert_add_fusion.sum_ref, f32[128,1152]{1,0:T(8,128)S(1)} %get-tuple-element.73.unit_ref, f32[128,128]{1,0:T(8,128)S(1)} %get-tuple-element.74.norm_ref, bf16[1152,1152]{1,0:T(8,128)(2,1)S(1)} %get-tuple-element.75.weight_ref, ...), custom_call_target="tpu_custom_call" | custom-call | flops 339738624 | bytes 5373952 | tf_op jit(solution)/shard_map/pallas_call | solution.py:70
  132.2 2.3 %collective-permute-done.33.refs_0_ = bf16[128,1152]{1,0:T(8,128)(2,1)S(1)} collective-permute-done((bf16[128,1152]{1,0:T(8,128)(2,1)S(1)}, bf16[128,1152]{1,0:T(8,128)(2,1)S(1)}, u32[]{:S(2)}, u32[]{:S(2)}) %collective-permute-start.33) | collective-permute-done | bytes 294944 | tf_op jit(solution)/shard_map/ppermute | solution.py:25
  134.4 1.8 %shard_map.66 = f32[128,1152]{1,0:T(8,128)} custom-call(s32[1]{0:T(128)} %bitcast.where_ref, f32[128,1152]{1,0:T(8,128)S(1)} %get-tuple-element.88.sum_ref, f32[128,1152]{1,0:T(8,128)S(1)} %get-tuple-element.89.unit_ref, f32[128,128]{1,0:T(8,128)S(1)} %get-tuple-element.90.norm_ref, bf16[1152,1152]{1,0:T(8,128)(2,1)S(1)} %get-tuple-element.91.weight_ref, ...), custom_call_target="tpu_custom_call" | custom-call | flops 339738624 | bytes 4784128 | tf_op jit(solution)/shard_map/pallas_call | solution.py:70
  (92 shorter events, 30.6 us)
Async XLA Ops:
  0.7 14.2 %collective-permute-start.4 = (bf16[128,1152]{1,0:T(8,128)(2,1)}, bf16[128,1152]{1,0:T(8,128)(2,1)S(1)}, u32[]{:S(2)}, u32[]{:S(2)}) collective-permute-start(bf16[128,1152]{1,0:T(8,128)(2,1)} %refs_8_.1), channel_id=1, source_target_pairs={{0,8},{1,9},{2,10},{3,11},{4,12},{5,13},{6,14},{7,15},{8,16},{9,17... | collective-permute-start | bytes 884744 | tf_op jit(solution)/shard_map/ppermute | solution.py:25
  3.7 6.0 %collective-permute-start.3 = (bf16[18,1152]{1,0:T(8,128)(2,1)S(1)}, bf16[18,1152]{1,0:T(8,128)(2,1)S(1)}, u32[]{:S(2)}, u32[]{:S(2)}) collective-permute-start(bf16[18,1152]{1,0:T(8,128)(2,1)S(1)} %pad_maximum_fusion.refs_0_), channel_id=1, source_target_pairs={{0,2},{2,4},{4,6},{6,0},{1,3},{3,5},{5,7},{7,1},{8,10},{10,12},{12... | collective-permute-start | bytes 124424 | tf_op jit(solution)/shard_map/ppermute | solution.py:21
  5.3 6.0 %collective-permute-start.2 = (bf16[18,1152]{1,0:T(8,128)(2,1)S(1)}, bf16[18,1152]{1,0:T(8,128)(2,1)S(1)}, u32[]{:S(2)}, u32[]{:S(2)}) collective-permute-start(bf16[18,1152]{1,0:T(8,128)(2,1)S(1)} %pad_maximum_fusion.refs_0_), channel_id=1, source_target_pairs={{0,4},{2,6},{4,0},{6,2},{1,5},{3,7},{5,1},{7,3},{8,12},{10,14},{12... | collective-permute-start | bytes 124424 | tf_op jit(solution)/shard_map/ppermute | solution.py:21
  8.2 4.2 %collective-permute-start.1 = (bf16[18,1152]{1,0:T(8,128)(2,1)S(1)}, bf16[18,1152]{1,0:T(8,128)(2,1)S(1)}, u32[]{:S(2)}, u32[]{:S(2)}) collective-permute-start(bf16[18,1152]{1,0:T(8,128)(2,1)S(1)} %pad_maximum_fusion.refs_0_), channel_id=1, source_target_pairs={{0,6},{2,0},{4,2},{6,4},{1,7},{3,1},{5,3},{7,5},{8,14},{10,8},{12,... | collective-permute-start | bytes 124424 | tf_op jit(solution)/shard_map/ppermute | solution.py:21
  14.9 20.6 %collective-permute-start.9 = (bf16[128,1280]{1,0:T(8,128)(2,1)S(1)}, bf16[128,1280]{1,0:T(8,128)(2,1)S(1)}, u32[]{:S(2)}, u32[]{:S(2)}) collective-permute-start(bf16[128,1280]{1,0:T(8,128)(2,1)S(1)} %fusion.1.refs_8_), channel_id=1, source_target_pairs={{0,2},{2,4},{4,6},{6,0},{1,3},{3,5},{5,7},{7,1},{8,10},{10,12},{12... | collective-permute-start | bytes 983048 | tf_op jit(solution)/shard_map/ppermute | solution.py:21
  16.5 19.8 %collective-permute-start.8 = (bf16[128,1280]{1,0:T(8,128)(2,1)S(1)}, bf16[128,1280]{1,0:T(8,128)(2,1)S(1)}, u32[]{:S(2)}, u32[]{:S(2)}) collective-permute-start(bf16[128,1280]{1,0:T(8,128)(2,1)S(1)} %fusion.1.refs_8_), channel_id=1, source_target_pairs={{0,4},{2,6},{4,0},{6,2},{1,5},{3,7},{5,1},{7,3},{8,12},{10,14},{12... | collective-permute-start | bytes 983048 | tf_op jit(solution)/shard_map/ppermute | solution.py:21
  19.4 17.6 %collective-permute-start.7 = (bf16[128,1280]{1,0:T(8,128)(2,1)S(1)}, bf16[128,1280]{1,0:T(8,128)(2,1)S(1)}, u32[]{:S(2)}, u32[]{:S(2)}) collective-permute-start(bf16[128,1280]{1,0:T(8,128)(2,1)S(1)} %fusion.1.refs_8_), channel_id=1, source_target_pairs={{0,6},{2,0},{4,2},{6,4},{1,7},{3,1},{5,3},{7,5},{8,14},{10,8},{12,... | collective-permute-start | bytes 983048 | tf_op jit(solution)/shard_map/ppermute | solution.py:21
  20.8 14.8 %collective-permute-start.6 = (bf16[128,1152]{1,0:T(8,128)(2,1)S(1)}, bf16[128,1152]{1,0:T(8,128)(2,1)S(1)}, u32[]{:S(2)}, u32[]{:S(2)}) collective-permute-start(bf16[128,1152]{1,0:T(8,128)(2,1)S(1)} %collective-permute-done.4.refs_9_), channel_id=1, source_target_pairs={{0,8},{1,9},{2,10},{3,11},{4,12},{5,13},{6,14},{7,15},{8,16},{9,17... | collective-permute-start | bytes 884744 | tf_op jit(solution)/shard_map/ppermute | solution.py:25
  21.5 10.3 %collective-permute-start.5 = (bf16[72,1152]{1,0:T(8,128)(2,1)S(1)}, bf16[72,1152]{1,0:T(8,128)(2,1)S(1)}, u32[]{:S(2)}, u32[]{:S(2)}) collective-permute-start(bf16[72,1152]{1,0:T(8,128)(2,1)S(1)} %shard_map.59), channel_id=1, source_target_pairs={{0,232},{1,224},{2,248},{3,208},{4,192},{5,200},{6,240},{7,216},{8... | collective-permute-start | bytes 497672 | tf_op jit(solution)/shard_map/ppermute | solution.py:108
  37.7 10.9 %collective-permute-start.10 = (bf16[128,1152]{1,0:T(8,128)(2,1)S(1)}, bf16[128,1152]{1,0:T(8,128)(2,1)S(1)}, u32[]{:S(2)}, u32[]{:S(2)}) collective-permute-start(bf16[128,1152]{1,0:T(8,128)(2,1)S(1)} %collective-permute-done.6.refs_10_), channel_id=1, source_target_pairs={{0,8},{1,9},{2,10},{3,11},{4,12},{5,13},{6,14},{7,15},{8,16},{9,17... | collective-permute-start | bytes 884744 | tf_op jit(solution)/shard_map/ppermute | solution.py:25
  38.5 6.6 %collective-permute-start.13 = (bf16[72,1152]{1,0:T(8,128)(2,1)S(1)}, bf16[72,1152]{1,0:T(8,128)(2,1)S(1)}, u32[]{:S(2)}, u32[]{:S(2)}) collective-permute-start(bf16[72,1152]{1,0:T(8,128)(2,1)S(1)} %collective-permute-done.5.refs_0_), channel_id=1, source_target_pairs={{6,0},{193,1},{0,2},{195,3},{2,4},{197,5},{4,6},{199,7},{14,8},{20... | collective-permute-start | bytes 497672 | tf_op jit(solution)/shard_map/ppermute | solution.py:44
  38.5 8.8 %collective-permute-start.12 = (bf16[72,1152]{1,0:T(8,128)(2,1)S(1)}, bf16[72,1152]{1,0:T(8,128)(2,1)S(1)}, u32[]{:S(2)}, u32[]{:S(2)}) collective-permute-start(bf16[72,1152]{1,0:T(8,128)(2,1)S(1)} %collective-permute-done.5.refs_0_), channel_id=1, source_target_pairs={{4,0},{129,1},{6,2},{131,3},{0,4},{133,5},{2,6},{135,7},{12,8},{13... | collective-permute-start | bytes 497672 | tf_op jit(solution)/shard_map/ppermute | solution.py:44
  42.2 5.5 %collective-permute-start.11 = (bf16[72,1152]{1,0:T(8,128)(2,1)S(1)}, bf16[72,1152]{1,0:T(8,128)(2,1)S(1)}, u32[]{:S(2)}, u32[]{:S(2)}) collective-permute-start(bf16[72,1152]{1,0:T(8,128)(2,1)S(1)} %collective-permute-done.5.refs_0_), channel_id=1, source_target_pairs={{2,0},{65,1},{4,2},{67,3},{6,4},{69,5},{0,6},{71,7},{10,8},{73,9},... | collective-permute-start | bytes 497672 | tf_op jit(solution)/shard_map/ppermute | solution.py:44
  49.5 20.5 %collective-permute-start.18 = (bf16[288,1152]{1,0:T(8,128)(2,1)S(1)}, bf16[288,1152]{1,0:T(8,128)(2,1)S(1)}, u32[]{:S(2)}, u32[]{:S(2)}) collective-permute-start(bf16[288,1152]{1,0:T(8,128)(2,1)S(1)} %shard_map.60.refs_0_), channel_id=1, source_target_pairs={{192,0},{7,1},{194,2},{1,3},{196,4},{3,5},{198,6},{5,7},{200,8},{1... | collective-permute-start | bytes 1990664 | tf_op jit(solution)/shard_map/ppermute | solution.py:44
  51.4 24.2 %collective-permute-start.17 = (bf16[288,1152]{1,0:T(8,128)(2,1)S(1)}, bf16[288,1152]{1,0:T(8,128)(2,1)S(1)}, u32[]{:S(2)}, u32[]{:S(2)}) collective-permute-start(bf16[288,1152]{1,0:T(8,128)(2,1)S(1)} %shard_map.60.refs_0_), channel_id=1, source_target_pairs={{128,0},{5,1},{130,2},{7,3},{132,4},{1,5},{134,6},{3,7},{136,8},{1... | collective-permute-start | bytes 1990664 | tf_op jit(solution)/shard_map/ppermute | solution.py:44
  52.8 22.8 %collective-permute-start.16 = (bf16[288,1152]{1,0:T(8,128)(2,1)S(1)}, bf16[288,1152]{1,0:T(8,128)(2,1)S(1)}, u32[]{:S(2)}, u32[]{:S(2)}) collective-permute-start(bf16[288,1152]{1,0:T(8,128)(2,1)S(1)} %shard_map.60.refs_0_), channel_id=1, source_target_pairs={{64,0},{3,1},{66,2},{5,3},{68,4},{7,5},{70,6},{1,7},{72,8},{11,9},... | collective-permute-start | bytes 1990664 | tf_op jit(solution)/shard_map/ppermute | solution.py:44
  54.2 21.4 %collective-permute-start.15 = (bf16[288,1152]{1,0:T(8,128)(2,1)S(1)}, bf16[288,1152]{1,0:T(8,128)(2,1)S(1)}, u32[]{:S(2)}, u32[]{:S(2)}) collective-permute-start(bf16[288,1152]{1,0:T(8,128)(2,1)S(1)} %shard_map.60.refs_0_), channel_id=1, source_target_pairs={{0,1},{1,0},{2,3},{3,2},{4,5},{5,4},{6,7},{7,6},{8,9},{9,8},{10,11... | collective-permute-start | bytes 1990664 | tf_op jit(solution)/shard_map/ppermute | solution.py:21
  56.1 13.2 %collective-permute-start.14 = (bf16[128,1152]{1,0:T(8,128)(2,1)}, bf16[128,1152]{1,0:T(8,128)(2,1)S(1)}, u32[]{:S(2)}, u32[]{:S(2)}) collective-permute-start(bf16[128,1152]{1,0:T(8,128)(2,1)} %copy-done.13), channel_id=1, source_target_pairs={{0,8},{1,9},{2,10},{3,11},{4,12},{5,13},{6,14},{7,15},{8,16},{9,17... | collective-permute-start | bytes 884744 | tf_op jit(solution)/shard_map/ppermute | solution.py:25
  75.6 3.2 %collective-permute-start.20 = (bf16[288,1152]{1,0:T(8,128)(2,1)S(1)}, bf16[288,1152]{1,0:T(8,128)(2,1)}, u32[]{:S(2)}, u32[]{:S(2)}) collective-permute-start(bf16[288,1152]{1,0:T(8,128)(2,1)S(1)} %collective-permute-done.17.refs_2_), channel_id=1, source_target_pairs={{0,1},{1,0},{2,3},{3,2},{4,5},{5,4},{6,7},{7,6},{8,9},{9,8},{10,11... | collective-permute-start | bytes 1990664 | tf_op jit(solution)/shard_map/ppermute | solution.py:21
  76.1 3.6 %collective-permute-start.21 = (bf16[288,1152]{1,0:T(8,128)(2,1)S(1)}, bf16[288,1152]{1,0:T(8,128)(2,1)}, u32[]{:S(2)}, u32[]{:S(2)}) collective-permute-start(bf16[288,1152]{1,0:T(8,128)(2,1)S(1)} %collective-permute-done.18.refs_3_), channel_id=1, source_target_pairs={{0,1},{1,0},{2,3},{3,2},{4,5},{5,4},{6,7},{7,6},{8,9},{9,8},{10,11... | collective-permute-start | bytes 1990664 | tf_op jit(solution)/shard_map/ppermute | solution.py:21
  87.3 5.9 %collective-permute-start.22 = (bf16[512,1280]{1,0:T(8,128)(2,1)S(1)}, bf16[512,1280]{1,0:T(8,128)(2,1)S(1)}, u32[]{:S(2)}, u32[]{:S(2)}) collective-permute-start(bf16[512,1280]{1,0:T(8,128)(2,1)S(1)} %get-tuple-element.66.own_emb), channel_id=1, source_target_pairs={{0,1},{1,0},{2,3},{3,2},{4,5},{5,4},{6,7},{7,6},{8,9},{9,8},{10,11... | collective-permute-start | bytes 3932168 | tf_op jit(solution)/shard_map/ppermute | solution.py:21
  96.8 8.5 %collective-permute-start.24 = (bf16[128,1152]{1,0:T(8,128)(2,1)S(1)}, bf16[128,1152]{1,0:T(8,128)(2,1)S(1)}, u32[]{:S(2)}, u32[]{:S(2)}) collective-permute-start(bf16[128,1152]{1,0:T(8,128)(2,1)S(1)} %get-tuple-element.76), channel_id=1, source_target_pairs={{0,248},{1,249},{2,250},{3,251},{4,252},{5,253},{6,254},{7,255},{8... | collective-permute-start | bytes 884744 | tf_op jit(solution)/shard_map/ppermute | solution.py:25
  100.7 29.5 %collective-permute-start.23 = (bf16[128,1152]{1,0:T(8,128)(2,1)S(1)}, bf16[128,1152]{1,0:T(8,128)(2,1)S(1)}, u32[]{:S(2)}, u32[]{:S(2)}) collective-permute-start(bf16[128,1152]{1,0:T(8,128)(2,1)S(1)} %get-tuple-element.72), channel_id=1, source_target_pairs={{0,1},{1,0},{2,3},{3,2},{4,5},{5,4},{6,7},{7,6},{8,9},{9,8},{10,11... | collective-permute-start | bytes 884744 | tf_op jit(solution)/shard_map/ppermute | solution.py:21
  100.8 8.2 %collective-permute-start.26 = (bf16[128,1152]{1,0:T(8,128)(2,1)S(1)}, bf16[128,1152]{1,0:T(8,128)(2,1)S(1)}, u32[]{:S(2)}, u32[]{:S(2)}) collective-permute-start(bf16[128,1152]{1,0:T(8,128)(2,1)S(1)} %get-tuple-element.79), channel_id=1, source_target_pairs={{0,1},{1,0},{2,3},{3,2},{4,5},{5,4},{6,7},{7,6},{8,9},{9,8},{10,11... | collective-permute-start | bytes 884744 | tf_op jit(solution)/shard_map/ppermute | solution.py:21
  101.3 18.7 %collective-permute-start.28 = (bf16[128,1152]{1,0:T(8,128)(2,1)S(1)}, bf16[128,1152]{1,0:T(8,128)(2,1)S(1)}, u32[]{:S(2)}, u32[]{:S(2)}) collective-permute-start(bf16[128,1152]{1,0:T(8,128)(2,1)S(1)} %get-tuple-element.82), channel_id=1, source_target_pairs={{0,1},{1,0},{2,3},{3,2},{4,5},{5,4},{6,7},{7,6},{8,9},{9,8},{10,11... | collective-permute-start | bytes 884744 | tf_op jit(solution)/shard_map/ppermute | solution.py:21
  101.4 9.5 %collective-permute-start.31 = (bf16[128,1152]{1,0:T(8,128)(2,1)S(1)}, bf16[128,1152]{1,0:T(8,128)(2,1)S(1)}, u32[]{:S(2)}, u32[]{:S(2)}) collective-permute-start(bf16[128,1152]{1,0:T(8,128)(2,1)S(1)} %get-tuple-element.86), channel_id=1, source_target_pairs={{0,1},{1,0},{2,3},{3,2},{4,5},{5,4},{6,7},{7,6},{8,9},{9,8},{10,11... | collective-permute-start | bytes 884744 | tf_op jit(solution)/shard_map/ppermute | solution.py:21
  105.3 8.7 %collective-permute-start.25 = (bf16[128,1152]{1,0:T(8,128)(2,1)S(1)}, bf16[128,1152]{1,0:T(8,128)(2,1)S(1)}, u32[]{:S(2)}, u32[]{:S(2)}) collective-permute-start(bf16[128,1152]{1,0:T(8,128)(2,1)S(1)} %add_convert_fusion.5), channel_id=1, source_target_pairs={{0,248},{1,249},{2,250},{3,251},{4,252},{5,253},{6,254},{7,255},{8... | collective-permute-start | bytes 884744 | tf_op jit(solution)/shard_map/ppermute | solution.py:25
  109.1 8.6 %collective-permute-start.27 = (bf16[128,1152]{1,0:T(8,128)(2,1)S(1)}, bf16[128,1152]{1,0:T(8,128)(2,1)S(1)}, u32[]{:S(2)}, u32[]{:S(2)}) collective-permute-start(bf16[128,1152]{1,0:T(8,128)(2,1)S(1)} %add_convert_fusion.4), channel_id=1, source_target_pairs={{0,2},{2,4},{4,6},{6,0},{1,3},{3,5},{5,7},{7,1},{8,10},{10,12},{12... | collective-permute-start | bytes 884744 | tf_op jit(solution)/shard_map/ppermute | solution.py:21
  111.0 10.7 %collective-permute-start.32 = (bf16[128,1152]{1,0:T(8,128)(2,1)S(1)}, bf16[128,1152]{1,0:T(8,128)(2,1)S(1)}, u32[]{:S(2)}, u32[]{:S(2)}) collective-permute-start(bf16[128,1152]{1,0:T(8,128)(2,1)S(1)} %add_convert_fusion.1), channel_id=1, source_target_pairs={{0,6},{2,0},{4,2},{6,4},{1,7},{3,1},{5,3},{7,5},{8,14},{10,8},{12,... | collective-permute-start | bytes 884744 | tf_op jit(solution)/shard_map/ppermute | solution.py:21
  117.7 7.4 %collective-permute-start.30 = (bf16[128,1152]{1,0:T(8,128)(2,1)S(1)}, bf16[128,1152]{1,0:T(8,128)(2,1)S(1)}, u32[]{:S(2)}, u32[]{:S(2)}) collective-permute-start(bf16[128,1152]{1,0:T(8,128)(2,1)S(1)} %add_convert_fusion.2), channel_id=1, source_target_pairs={{0,248},{1,249},{2,250},{3,251},{4,252},{5,253},{6,254},{7,255},{8... | collective-permute-start | bytes 884744 | tf_op jit(solution)/shard_map/ppermute | solution.py:25
  120.1 10.2 %collective-permute-start.29 = (bf16[128,1152]{1,0:T(8,128)(2,1)S(1)}, bf16[128,1152]{1,0:T(8,128)(2,1)S(1)}, u32[]{:S(2)}, u32[]{:S(2)}) collective-permute-start(bf16[128,1152]{1,0:T(8,128)(2,1)S(1)} %add_convert_fusion.3), channel_id=1, source_target_pairs={{0,4},{2,6},{4,0},{6,2},{1,5},{3,7},{5,1},{7,3},{8,12},{10,14},{12... | collective-permute-start | bytes 884744 | tf_op jit(solution)/shard_map/ppermute | solution.py:21
  125.1 9.3 %collective-permute-start.33 = (bf16[128,1152]{1,0:T(8,128)(2,1)S(1)}, bf16[128,1152]{1,0:T(8,128)(2,1)S(1)}, u32[]{:S(2)}, u32[]{:S(2)}) collective-permute-start(bf16[128,1152]{1,0:T(8,128)(2,1)S(1)} %add_convert_fusion), channel_id=1, source_target_pairs={{0,248},{1,249},{2,250},{3,251},{4,252},{5,253},{6,254},{7,255},{8... | collective-permute-start | bytes 884744 | tf_op jit(solution)/shard_map/ppermute | solution.py:25
  (19 other events, 53.4 us)
where the time goes:
time: 139 us; the launch traced here: 136 us
  waiting for transfers between devices  54.7 us (39%)
  starting transfers between devices  48.4 us (35%)
  Pallas kernels  20.2 us (15%)
  local copies, waits for them, and re-layouts  9.12 us (7%)
  other arithmetic  3.06 us (2%)
    ppermute x8, waiting for transfers between devices, blocks_behind(): lax.ppermute(value, AXES, [(i, (i + steps) % 256) for i in range(256)])  30.2 us
    ppermute x19, starting transfers between devices, along(): lax.ppermute(value, axis, [(i, (i + steps) % count) for i in range(count)])  21.5 us
    pallas_call x8, Pallas kernels, on_device(): pl.pallas_call(body, out_shape=outs, in_specs=[pl.BlockSpec(memory_space=...  20.2 us
    ppermute x8, starting transfers between devices, blocks_behind(): lax.ppermute(value, AXES, [(i, (i + steps) % 256) for i in range(256)])  11.8 us
    ppermute x6, waiting for transfers between devices, crosswise(): return lax.ppermute(value, AXES, pairs)  10.1 us
    ppermute x19, waiting for transfers between devices, along(): lax.ppermute(value, axis, [(i, (i + steps) % count) for i in range(count)])  9.78 us
    ppermute x6, starting transfers between devices, crosswise(): return lax.ppermute(value, AXES, pairs)  9.51 us
    unnamed x34, local copies, waits for them, and re-layouts  8.98 us
  transfers between devices with their start and end apart: 34, of which 19 were waited for; matrix products, arithmetic and copies ran while one was open for 2% of the time, Pallas kernels for 8%

commit v1 on v0

--- a/solution.py
+++ b/solution.py
@@ -71,7 +71,8 @@
         body,
         out_shape=outs,
         in_specs=[pl.BlockSpec(memory_space=pltpu.SMEM)]
-        + [pl.BlockSpec(memory_space=pl.ANY)] * anywhere
+        + [pl.BlockSpec(memory_space=pl.ANY)] * min(anywhere, 8)
+        + [pl.BlockSpec(memory_space=pltpu.HBM)] * max(anywhere - 8, 0)
         + [pl.BlockSpec(memory_space=pltpu.VMEM)] * (len(arrays) - anywhere),
         out_specs=[pl.BlockSpec(memory_space=pltpu.VMEM)] * len(outs),
         scratch_shapes=list(scratch),
@@ -141,32 +142,45 @@
                 copy.wait()
 
 
-def embed(sources, weight, emb, unit_ref, norm_ref):
+def bring(sources, held, sems):
+    rows = sources[0].shape[0]
+    copies = [
+        pltpu.make_async_copy(source, held.at[pl.ds(n * rows, rows)], sems.at[n]) for n, source in enumerate(sources)
+    ]
+    for copy in copies:
+        copy.start()
+    return copies
+
+
+def embed(held, weight, emb, unit_ref, norm_ref):
     rows, width = unit_ref.shape
-    for first in range(0, len(sources), 2):
-        some = sources[first : first + 2]
-        features = jnp.concatenate([source[:, :width] for source in some])
-        unit, norm = normalize(jnp.dot(features, weight[...], preferred_element_type=jnp.float32))
-        emb[pl.ds(first * rows, len(some) * rows), :width] = unit.astype(jnp.bfloat16)
+    for first in range(0, held.shape[0], 2 * rows):
+        at = slice(first, min(first + 2 * rows, held.shape[0]))
+        unit, norm = normalize(jnp.dot(held[at, :width], weight[...], preferred_element_type=jnp.float32))
+        emb[at, :width] = unit.astype(jnp.bfloat16)
         if first == 0:
             unit_ref[...] = unit[:rows]
             norm_ref[...] = jnp.broadcast_to(norm[:rows], norm_ref.shape)
 
 
 def embed_images(where_ref, *refs):
-    weight, emb, unit_ref, norm_ref, sems = refs[12:]
+    weight, emb, unit_ref, norm_ref, sems, held, held_sems = refs[12:]
+    copies = bring(refs[8:12], held, held_sems)
     place(where_ref, True, refs[:8], weight, sems)
-    images = refs[8:12]
-    embed(images, weight, emb, unit_ref, norm_ref)
-    rows, width = unit_ref.shape
-    for slot, image in enumerate(images):
-        emb[slot * rows : (slot + 1) * rows, width:] = image[:, width:]
+    for copy in copies:
+        copy.wait()
+    embed(held, weight, emb, unit_ref, norm_ref)
+    width = unit_ref.shape[1]
+    emb[:, width:] = held[:, width:]
 
 
 def embed_texts(where_ref, *refs):
-    weight, emb, unit_ref, norm_ref, sems = refs[13:]
+    weight, emb, unit_ref, norm_ref, sems, held, held_sems = refs[13:]
+    copies = bring(refs[8:13], held, held_sems)
     place(where_ref, False, refs[:8], weight, sems)
-    embed(refs[8:13], weight, emb, unit_ref, norm_ref)
+    for copy in copies:
+        copy.wait()
+    embed(held, weight, emb, unit_ref, norm_ref)
 
 
 def text_sum(own_coeff, other_coeff, own_emb, other_emb, plane):
@@ -181,45 +195,61 @@
     return total
 
 
-def weigh_pairs(where_ref, own_emb, other_emb, text_emb, own_coeff, other_coeff, far_ref):
-    core, y = where_ref[0], where_ref[3]
-    rows, width = text_emb.shape[0] // 5, text_emb.shape[1]
+def weigh(where_ref, kind, emb, text_emb, coeff_ref, planes):
+    core, y = where_ref[0], where_ref[1]
+    rows, width = emb.shape[0] // 4, text_emb.shape[1]
     column = lax.broadcasted_iota(jnp.int32, (rows, rows), 1)
-    for kind, (emb, coeff_ref) in enumerate(((own_emb, own_coeff), (other_emb, other_coeff))):
-        for first in (0, 2):
-            logits = logit_bias + logit_scale * lax.dot_general(
-                emb[first * rows : (first + 2) * rows, :width], text_emb[...], contract_last,
-                preferred_element_type=jnp.float32,
-            )
-            chance = jax.nn.sigmoid(logits)
-            for slot in (first, first + 1):
-                ahead = 2 * lax.rem(y + slot, 4) + lax.rem(core + kind, 2)
-                at = slice(slot * rows, (slot + 1) * rows)
-                marks = emb[at, width:].astype(jnp.float32).astype(jnp.int32)
-                behind, label = marks[:, 0:1], marks[:, 1:2]
-                hit = column == label
-                for plane in range(WINDOW_PLANES + 1):
-                    distance = ahead + 8 * plane - (2 * y + core)
-                    columns = slice(plane * rows, (plane + 1) * rows)
-                    tile = chance[(slot - first) * rows : (slot - first + 1) * rows, columns]
-                    tile = tile - jnp.where(hit & (behind == distance), 1.0, 0.0)
-                    if plane in (0, WINDOW_PLANES):
-                        tile = tile * jnp.where((distance >= 0) & (distance < 8 * WINDOW_PLANES), 1.0, 0.0)
-                    coeff_ref[at, columns] = tile.astype(jnp.bfloat16)
-    far_ref[...] = text_sum(own_coeff, other_coeff, own_emb, other_emb, WINDOW_PLANES).astype(far_ref.dtype)
-
-
-def sum_pairs(where_ref, own_coeff, other_coeff, own_emb, other_emb, text_emb, *outs):
+    texts = text_emb[planes[0] * rows : (planes[-1] + 1) * rows, :]
+    for first in (0, 2):
+        logits = logit_bias + logit_scale * lax.dot_general(
+            emb[first * rows : (first + 2) * rows, :width], texts, contract_last, preferred_element_type=jnp.float32
+        )
+        chance = jax.nn.sigmoid(logits)
+        for slot in (first, first + 1):
+            ahead = 2 * lax.rem(y + slot, 4) + lax.rem(core + kind, 2)
+            at = slice(slot * rows, (slot + 1) * rows)
+            marks = emb[at, width:].astype(jnp.float32).astype(jnp.int32)
+            behind, label = marks[:, 0:1], marks[:, 1:2]
+            hit = column == label
+            for n, plane in enumerate(planes):
+                distance = ahead + 8 * plane - (2 * y + core)
+                columns = slice(n * rows, (n + 1) * rows)
+                tile = chance[(slot - first) * rows : (slot - first + 1) * rows, columns]
+                tile = tile - jnp.where(hit & (behind == distance), 1.0, 0.0)
+                if plane in (0, WINDOW_PLANES):
+                    tile = tile * jnp.where((distance >= 0) & (distance < 8 * WINDOW_PLANES), 1.0, 0.0)
+                coeff_ref[at, columns] = tile.astype(jnp.bfloat16)
+
+
+def sum_far(where_ref, own_emb, other_emb, text_emb, own_coeff, other_coeff, third_ref, far_ref):
+    planes = (WINDOW_PLANES - 1, WINDOW_PLANES)
+    weigh(where_ref, 0, own_emb, text_emb, own_coeff, planes)
+    weigh(where_ref, 1, other_emb, text_emb, other_coeff, planes)
+    for n, sum_ref in enumerate((third_ref, far_ref)):
+        sum_ref[...] = text_sum(own_coeff, other_coeff, own_emb, other_emb, n).astype(sum_ref.dtype)
+
+
+def sum_pairs(where_ref, own_far, other_far, own_emb, other_emb, text_emb, *refs):
     rows = own_emb.shape[0] // 4
-    text_sums, kept, sent = outs[:4], outs[4:8], outs[8:]
-    for plane in range(WINDOW_PLANES):
+    text_sums, kept, sent = refs[:3], refs[3:7], refs[7:11]
+    own_coeff, other_coeff = refs[11:]
+    planes = tuple(range(WINDOW_PLANES - 1))
+    near = len(planes) * rows
+    weigh(where_ref, 0, own_emb, text_emb, own_coeff, planes)
+    weigh(where_ref, 1, other_emb, text_emb, other_coeff, planes)
+    for plane in planes:
         text_sums[plane][...] = text_sum(own_coeff, other_coeff, own_emb, other_emb, plane)
+
+    def image_sum(coeff, far, at):
+        total = jnp.dot(coeff[at, :], text_emb[:near, :], preferred_element_type=jnp.float32)
+        return total + jnp.dot(far[at, :], text_emb[near:, :], preferred_element_type=jnp.float32)
+
     for first in (0, 2):
         at = slice(first * rows, (first + 2) * rows)
-        both = jnp.dot(own_coeff[at, :], text_emb[...], preferred_element_type=jnp.float32)
+        both = image_sum(own_coeff, own_far, at)
         kept[first][...] = both[:rows]
         kept[first + 1][...] = both[rows:]
-        both = jnp.dot(other_coeff[at, :], text_emb[...], preferred_element_type=jnp.float32)
+        both = image_sum(other_coeff, other_far, at)
         sent[first][...] = both[:rows].astype(jnp.bfloat16)
         sent[first + 1][...] = both[rows:].astype(jnp.bfloat16)
 
@@ -231,6 +261,14 @@
         total = total + one[...].astype(jnp.float32)
     draw = unproject(unit_ref[...], norm_ref[:, 0:1], logit_scale * total)
     grad_ref[...] = lax.dot_general(draw, weight_ref[...], contract_last, preferred_element_type=jnp.float32)
+
+
+def last_step_home(value):
+    pairs = []
+    for x, z, y, c in everyone():
+        first_z = (z - 3) % 8
+        pairs.append((device(x, z, y, c), device((x if first_z >= 4 else x - 1) % 4, (z + 1) % 8, y, c)))
+    return lax.ppermute(value, AXES, pairs)
 
 
 def normalize(raw):
@@ -274,37 +312,39 @@
     low = jnp.bfloat16
     sems = [pltpu.SemaphoreType.DMA((4,))]
     image_weight, image_emb, image_unit, image_norm = on_device(
-        embed_images, where, pieces + images, [whole, like(4 * rows, width + 128, low), wide, narrow], sems,
-        flops=8 * rows * width * width, vmem=16, anywhere=8,
+        embed_images, where, pieces + images, [whole, like(4 * rows, width + 128, low), wide, narrow],
+        [*sems, pltpu.VMEM((4 * rows, width + 128), low), pltpu.SemaphoreType.DMA((4,))],
+        flops=8 * rows * width * width, vmem=56, anywhere=12,
     )
     other_emb = along(image_emb, "c", 1)
     text_weight, text_emb, text_unit, text_norm = on_device(
-        embed_texts, where, pieces + texts, [whole, like(5 * rows, width, low), wide, narrow], sems,
-        flops=10 * rows * width * width, vmem=16, anywhere=8,
-    )
-    coeff, other_coeff, far = on_device(
-        weigh_pairs, where, [image_emb, other_emb, text_emb],
-        [like(4 * rows, 5 * rows, low), like(4 * rows, 5 * rows, low), like(rows, width, low)],
-        flops=96 * rows * rows * width, vmem=20,
-    )
-    far = blocks_behind(far, -8)
+        embed_texts, where, pieces + texts, [whole, like(5 * rows, width, low), wide, narrow],
+        [*sems, pltpu.VMEM((5 * rows, width), low), pltpu.SemaphoreType.DMA((5,))],
+        flops=10 * rows * width * width, vmem=56, anywhere=13,
+    )
+    own_far, other_far, third, far = on_device(
+        sum_far, (c, y), [image_emb, other_emb, text_emb],
+        [like(4 * rows, 2 * rows, low)] * 2 + [like(rows, width, low)] * 2,
+        flops=64 * rows * rows * width, vmem=16,
+    )
+    home = along(far, "z", 3)
+    third = blocks_behind(third, -8)
     sums = on_device(
-        sum_pairs, (y,), [coeff, other_coeff, image_emb, other_emb, text_emb],
-        [wide] * 8 + [like(rows, width, low)] * 4,
-        flops=2 * 72 * rows * rows * width, vmem=20,
-    )
-    text_sums, kept, sent = sums[:4], sums[4:8], sums[8:]
-
-    far = blocks_behind((far.astype(jnp.float32) + text_sums[3]).astype(low), -8)
+        sum_pairs, (c, y), [own_far, other_far, image_emb, other_emb, text_emb],
+        [wide] * 7 + [like(rows, width, low)] * 4, [pltpu.VMEM((4 * rows, 3 * rows), low)] * 2,
+        flops=2 * 88 * rows * rows * width, vmem=20,
+    )
+    text_sums, kept, sent = sums[:3], sums[3:7], sums[7:]
+
+    second = blocks_behind((third.astype(jnp.float32) + text_sums[2]).astype(low), -8)
     chip = [kept[dy] + along(sent[dy], "c", 1).astype(jnp.float32) for dy in range(4)]
     arrived = [along(chip[dy].astype(low), "y", steps) for dy, steps in ((1, 1), (2, 2), (3, -1))]
-    far, arrived[0] = tied((far, arrived[0]))
-    far = blocks_behind((far.astype(jnp.float32) + text_sums[2]).astype(low), -8)
-    far, arrived[2] = tied((far, arrived[2]))
-    far = blocks_behind((far.astype(jnp.float32) + text_sums[1]).astype(low), -8)
+    home = last_step_home(home)
+    second, arrived[0] = tied((second, arrived[0]))
+    first = blocks_behind((second.astype(jnp.float32) + text_sums[1]).astype(low), -8)
     flops = 2 * rows * width * width
     (image_grad,) = on_device(finish, (y,), [chip[0], image_unit, image_norm, image_weight, *arrived], [wide], flops=flops, vmem=16)
-    (text_grad,) = on_device(finish, (y,), [text_sums[0], text_unit, text_norm, text_weight, far], [wide], flops=flops, vmem=16)
+    (text_grad,) = on_device(finish, (y,), [text_sums[0], text_unit, text_norm, text_weight, first, home], [wide], flops=flops, vmem=16)
     return (image_grad, text_grad)
 
 

time: 139 us -> 134 us (0.964); the launches traced: 136 us -> 133 us
  local copies, waits for them, and re-layouts: 9.12 us -> 2.13 us
  Pallas kernels: 20.2 us -> 25.6 us
  starting transfers between devices: 48.4 us -> 45.4 us
    ppermute x8 -> x7, starting transfers between devices: 11.8 us -> 4.19 us  [blocks_behind(): lax.ppermute(value, AXES, [(i, (i + steps) % 256) for i in range(256)])]
    unnamed x34 -> x44, local copies, waits for them, and re-layouts: 8.98 us -> 1.99 us
    pallas_call x8, Pallas kernels: 20.2 us -> 25.6 us  [on_device(): pl.pallas_call(body, out_shape=outs, in_specs=[pl.BlockSpec(memory_space=...]
    ppermute x8 -> x7, waiting for transfers between devices: 30.2 us -> 26.2 us  [blocks_behind(): lax.ppermute(value, AXES, [(i, (i + steps) % 256) for i in range(256)])]
    ppermute x19 -> x20, waiting for transfers between devices: 9.78 us -> 13.3 us  [along(): lax.ppermute(value, axis, [(i, (i + steps) % count) for i in range(count)])]
    ppermute x0 -> x1, starting transfers between devices: none -> 2.72 us  [last_step_home(): return lax.ppermute(value, AXES, pairs)]
    ppermute x19 -> x20, starting transfers between devices: 21.5 us -> 23.7 us  [along(): lax.ppermute(value, axis, [(i, (i + steps) % count) for i in range(count)])]
  transfers between devices with their start and end apart: 34 -> 35, of which waited for: 19 -> 20; matrix products, arithmetic and copies ran while one was open for 2% -> 3% of each run, Pallas kernels for 8% -> 11%
where the time goes in v1:
time: 134 us; the launch traced here: 133 us
  waiting for transfers between devices  55.7 us (42%)
  starting transfers between devices  45.4 us (34%)
  Pallas kernels  25.6 us (19%)
  other arithmetic  3.61 us (3%)
  local copies, waits for them, and re-layouts  2.13 us (2%)
    ppermute x7, waiting for transfers between devices, blocks_behind(): lax.ppermute(value, AXES, [(i, (i + steps) % 256) for i in range(256)])  26.2 us
    pallas_call x8, Pallas kernels, on_device(): pl.pallas_call(body, out_shape=outs, in_specs=[pl.BlockSpec(memory_space=...  25.6 us
    ppermute x20, starting transfers between devices, along(): lax.ppermute(value, axis, [(i, (i + steps) % count) for i in range(count)])  23.7 us
    ppermute x20, waiting for transfers between devices, along(): lax.ppermute(value, axis, [(i, (i + steps) % count) for i in range(count)])  13.3 us
    ppermute x6, waiting for transfers between devices, crosswise(): return lax.ppermute(value, AXES, pairs)  10.1 us
    ppermute x6, starting transfers between devices, crosswise(): return lax.ppermute(value, AXES, pairs)  9.16 us
    ppermute x1, starting transfers between devices, spread_units(): return lax.ppermute(unit, AXES, pairs)  5.63 us
    ppermute x1, waiting for transfers between devices, spread_units(): return lax.ppermute(unit, AXES, pairs)  5.28 us
  transfers between devices with their start and end apart: 35, of which 20 were waited for; matrix products, arithmetic and copies ran while one was open for 3% of the time, Pallas kernels for 11%

profile of v1, /device:TPU:0, one launch (start us, length us, event | category | flops | bytes accessed | tf_op | source)
XLA Modules:
  0.0 133.4 jit_solution(16002568940613379469)
XLA Ops:
  3.7 1.7 %collective-permute-start.3 = (bf16[18,1152]{1,0:T(8,128)(2,1)S(1)}, bf16[18,1152]{1,0:T(8,128)(2,1)S(1)}, u32[]{:S(2)}, u32[]{:S(2)}) collective-permute-start(bf16[18,1152]{1,0:T(8,128)(2,1)S(1)} %pad_maximum_fusion.refs_0_), channel_id=1, source_target_pairs={{0,2},{2,4},{4,6},{6,0},{1,3},{3,5},{5,7},{7,1},{8,10},{10,12},{12... | collective-permute-start | bytes 124424 | tf_op jit(solution)/shard_map/ppermute | solution.py:21
  5.3 2.9 %collective-permute-start.2 = (bf16[18,1152]{1,0:T(8,128)(2,1)S(1)}, bf16[18,1152]{1,0:T(8,128)(2,1)S(1)}, u32[]{:S(2)}, u32[]{:S(2)}) collective-permute-start(bf16[18,1152]{1,0:T(8,128)(2,1)S(1)} %pad_maximum_fusion.refs_0_), channel_id=1, source_target_pairs={{0,4},{2,6},{4,0},{6,2},{1,5},{3,7},{5,1},{7,3},{8,12},{10,14},{12... | collective-permute-start | bytes 124424 | tf_op jit(solution)/shard_map/ppermute | solution.py:21
  9.7 1.7 %collective-permute-done.2.refs_2_ = bf16[18,1152]{1,0:T(8,128)(2,1)S(1)} collective-permute-done((bf16[18,1152]{1,0:T(8,128)(2,1)S(1)}, bf16[18,1152]{1,0:T(8,128)(2,1)S(1)}, u32[]{:S(2)}, u32[]{:S(2)}) %collective-permute-start.2) | collective-permute-done | bytes 41504 | tf_op jit(solution)/shard_map/ppermute | solution.py:21
  13.1 1.8 %collective-permute-done.4.refs_9_ = bf16[128,1152]{1,0:T(8,128)(2,1)S(1)} collective-permute-done((bf16[128,1152]{1,0:T(8,128)(2,1)}, bf16[128,1152]{1,0:T(8,128)(2,1)S(1)}, u32[]{:S(2)}, u32[]{:S(2)}) %collective-permute-start.4) | collective-permute-done | bytes 294944 | tf_op jit(solution)/shard_map/ppermute | solution.py:25
  14.9 1.6 %collective-permute-start.9 = (bf16[128,1280]{1,0:T(8,128)(2,1)S(1)}, bf16[128,1280]{1,0:T(8,128)(2,1)S(1)}, u32[]{:S(2)}, u32[]{:S(2)}) collective-permute-start(bf16[128,1280]{1,0:T(8,128)(2,1)S(1)} %fusion.1.refs_8_), channel_id=1, source_target_pairs={{0,2},{2,4},{4,6},{6,0},{1,3},{3,5},{5,7},{7,1},{8,10},{10,12},{12... | collective-permute-start | bytes 983048 | tf_op jit(solution)/shard_map/ppermute | solution.py:21
  16.5 2.9 %collective-permute-start.8 = (bf16[128,1280]{1,0:T(8,128)(2,1)S(1)}, bf16[128,1280]{1,0:T(8,128)(2,1)S(1)}, u32[]{:S(2)}, u32[]{:S(2)}) collective-permute-start(bf16[128,1280]{1,0:T(8,128)(2,1)S(1)} %fusion.1.refs_8_), channel_id=1, source_target_pairs={{0,4},{2,6},{4,0},{6,2},{1,5},{3,7},{5,1},{7,3},{8,12},{10,14},{12... | collective-permute-start | bytes 983048 | tf_op jit(solution)/shard_map/ppermute | solution.py:21
  20.8 5.6 %collective-permute-start.5 = (bf16[72,1152]{1,0:T(8,128)(2,1)S(1)}, bf16[72,1152]{1,0:T(8,128)(2,1)S(1)}, u32[]{:S(2)}, u32[]{:S(2)}) collective-permute-start(bf16[72,1152]{1,0:T(8,128)(2,1)S(1)} %shard_map.59), channel_id=1, source_target_pairs={{0,232},{1,224},{2,248},{3,208},{4,192},{5,200},{6,240},{7,216},{8... | collective-permute-start | bytes 497672 | tf_op jit(solution)/shard_map/ppermute | solution.py:109
  26.4 5.3 %collective-permute-done.5.refs_0_ = bf16[72,1152]{1,0:T(8,128)(2,1)S(1)} collective-permute-done((bf16[72,1152]{1,0:T(8,128)(2,1)S(1)}, bf16[72,1152]{1,0:T(8,128)(2,1)S(1)}, u32[]{:S(2)}, u32[]{:S(2)}) %collective-permute-start.5) | collective-permute-done | bytes 165920 | tf_op jit(solution)/shard_map/ppermute | solution.py:109
  31.7 3.9 %collective-permute-done.6.refs_10_ = bf16[128,1152]{1,0:T(8,128)(2,1)S(1)} collective-permute-done((bf16[128,1152]{1,0:T(8,128)(2,1)S(1)}, bf16[128,1152]{1,0:T(8,128)(2,1)S(1)}, u32[]{:S(2)}, u32[]{:S(2)}) %collective-permute-start.6) | collective-permute-done | bytes 294944 | tf_op jit(solution)/shard_map/ppermute | solution.py:25
  35.8 3.6 %collective-permute-start.12 = (bf16[72,1152]{1,0:T(8,128)(2,1)S(1)}, bf16[72,1152]{1,0:T(8,128)(2,1)S(1)}, u32[]{:S(2)}, u32[]{:S(2)}) collective-permute-start(bf16[72,1152]{1,0:T(8,128)(2,1)S(1)} %collective-permute-done.5.refs_0_), channel_id=1, source_target_pairs={{4,0},{129,1},{6,2},{131,3},{0,4},{133,5},{2,6},{135,7},{12,8},{13... | collective-permute-start | bytes 497672 | tf_op jit(solution)/shard_map/ppermute | solution.py:44
  39.4 1.5 %collective-permute-start.11 = (bf16[72,1152]{1,0:T(8,128)(2,1)S(1)}, bf16[72,1152]{1,0:T(8,128)(2,1)S(1)}, u32[]{:S(2)}, u32[]{:S(2)}) collective-permute-start(bf16[72,1152]{1,0:T(8,128)(2,1)S(1)} %collective-permute-done.5.refs_0_), channel_id=1, source_target_pairs={{2,0},{65,1},{4,2},{67,3},{6,4},{69,5},{0,6},{71,7},{10,8},{73,9},... | collective-permute-start | bytes 497672 | tf_op jit(solution)/shard_map/ppermute | solution.py:44
  40.9 1.4 %collective-permute-done.13.refs_3_ = bf16[72,1152]{1,0:T(8,128)(2,1)S(1)} collective-permute-done((bf16[72,1152]{1,0:T(8,128)(2,1)S(1)}, bf16[72,1152]{1,0:T(8,128)(2,1)S(1)}, u32[]{:S(2)}, u32[]{:S(2)}) %collective-permute-start.13) | collective-permute-done | bytes 165920 | tf_op jit(solution)/shard_map/ppermute | solution.py:44
  42.4 2.1 %collective-permute-done.12.refs_2_ = bf16[72,1152]{1,0:T(8,128)(2,1)S(1)} collective-permute-done((bf16[72,1152]{1,0:T(8,128)(2,1)S(1)}, bf16[72,1152]{1,0:T(8,128)(2,1)S(1)}, u32[]{:S(2)}, u32[]{:S(2)}) %collective-permute-start.12) | collective-permute-done | bytes 165920 | tf_op jit(solution)/shard_map/ppermute | solution.py:44
  45.0 2.0 %collective-permute-done.10.refs_11_ = bf16[128,1152]{1,0:T(8,128)(2,1)S(1)} collective-permute-done((bf16[128,1152]{1,0:T(8,128)(2,1)S(1)}, bf16[128,1152]{1,0:T(8,128)(2,1)S(1)}, u32[]{:S(2)}, u32[]{:S(2)}) %collective-permute-start.10) | collective-permute-done | bytes 294944 | tf_op jit(solution)/shard_map/ppermute | solution.py:25
  50.2 1.5 %collective-permute-start.16 = (bf16[288,1152]{1,0:T(8,128)(2,1)S(1)}, bf16[288,1152]{1,0:T(8,128)(2,1)S(1)}, u32[]{:S(2)}, u32[]{:S(2)}) collective-permute-start(bf16[288,1152]{1,0:T(8,128)(2,1)S(1)} %shard_map.60.refs_0_), channel_id=1, source_target_pairs={{64,0},{3,1},{66,2},{5,3},{68,4},{7,5},{70,6},{1,7},{72,8},{11,9},... | collective-permute-start | bytes 1990664 | tf_op jit(solution)/shard_map/ppermute | solution.py:44
  51.7 2.1 %collective-permute-start.15 = (bf16[288,1152]{1,0:T(8,128)(2,1)S(1)}, bf16[288,1152]{1,0:T(8,128)(2,1)S(1)}, u32[]{:S(2)}, u32[]{:S(2)}) collective-permute-start(bf16[288,1152]{1,0:T(8,128)(2,1)S(1)} %shard_map.60.refs_0_), channel_id=1, source_target_pairs={{0,1},{1,0},{2,3},{3,2},{4,5},{5,4},{6,7},{7,6},{8,9},{9,8},{10,11... | collective-permute-start | bytes 1990664 | tf_op jit(solution)/shard_map/ppermute | solution.py:21
  53.8 13.5 %collective-permute-done.14.refs_12_ = bf16[128,1152]{1,0:T(8,128)(2,1)S(1)} collective-permute-done((bf16[128,1152]{1,0:T(8,128)(2,1)}, bf16[128,1152]{1,0:T(8,128)(2,1)S(1)}, u32[]{:S(2)}, u32[]{:S(2)}) %collective-permute-start.14) | collective-permute-done | bytes 294944 | tf_op jit(solution)/shard_map/ppermute | solution.py:25
  67.3 6.0 %collective-permute-done.17.refs_2_ = bf16[288,1152]{1,0:T(8,128)(2,1)S(1)} collective-permute-done((bf16[288,1152]{1,0:T(8,128)(2,1)S(1)}, bf16[288,1152]{1,0:T(8,128)(2,1)S(1)}, u32[]{:S(2)}, u32[]{:S(2)}) %collective-permute-start.17) | collective-permute-done | bytes 663584 | tf_op jit(solution)/shard_map/ppermute | solution.py:44
  77.6 6.1 %shard_map.61 = (bf16[1152,1152]{1,0:T(8,128)(2,1)}, bf16[512,1280]{1,0:T(8,128)(2,1)}, f32[128,1152]{1,0:T(8,128)}, f32[128,128]{1,0:T(8,128)}) custom-call(s32[4]{0:T(128)} %pad_add_fusion.1.where_ref, bf16[288,1152]{1,0:T(8,128)(2,1)} %copy-done, bf16[288,1152]{1,0:T(8,128)(2,1)} %copy-done.12, bf16[288,1152]{1,0:T(8,128)(2,1)} %copy-done.11, ...), custom_call_target="tpu_custom_call" | custom-call | flops 1358954496 | bytes 11239424 | tf_op jit(solution)/shard_map/pallas_call | solution.py:70
  84.1 6.8 %shard_map.62 = (bf16[1152,1152]{1,0:T(8,128)(2,1)}, bf16[640,1152]{1,0:T(8,128)(2,1)}, f32[128,1152]{1,0:T(8,128)}, f32[128,128]{1,0:T(8,128)}) custom-call(s32[4]{0:T(128)} %pad_add_fusion.1.where_ref, bf16[288,1152]{1,0:T(8,128)(2,1)} %copy-done, bf16[288,1152]{1,0:T(8,128)(2,1)} %copy-done.12, bf16[288,1152]{1,0:T(8,128)(2,1)} %copy-done.11, ...), custom_call_target="tpu_custom_call" | custom-call | flops 1698693120 | bytes 11567104 | tf_op jit(solution)/shard_map/pallas_call | solution.py:70
  92.3 2.4 %shard_map.63 = (bf16[512,256]{1,0:T(8,128)(2,1)S(1)}, bf16[512,256]{1,0:T(8,128)(2,1)S(1)}, bf16[128,1152]{1,0:T(8,128)(2,1)S(1)}, bf16[128,1152]{1,0:T(8,128)(2,1)S(1)}) custom-call(s32[2]{0:T(128)S(1)} %pad_add_fusion.where_ref, bf16[512,1280]{1,0:T(8,128)(2,1)S(1)} %copy-done.9, bf16[512,1280]{1,0:T(8,128)(2,1)S(1)} %collective-permute-done.22.other_emb, ...), custom_call_target="tpu_custom_call" | custom-call | flops 1207959552 | bytes 5210112 | tf_op jit(solution)/shard_map/pallas_call | solution.py:70
  95.1 5.6 %shard_map.64 = (f32[128,1152]{1,0:T(8,128)S(1)}, f32[128,1152]{1,0:T(8,128)S(1)}, f32[128,1152]{1,0:T(8,128)S(1)}, f32[128,1152]{1,0:T(8,128)S(1)}, f32[128,115...) custom-call(s32[2]{0:T(128)S(1)} %pad_add_fusion.where_ref, ...), custom_call_target="tpu_custom_call" | custom-call | flops 3321888768 | bytes 9928704 | tf_op jit(solution)/shard_map/pallas_call | solution.py:70
  101.7 2.4 %collective-permute-done.24 = bf16[128,1152]{1,0:T(8,128)(2,1)S(1)} collective-permute-done((bf16[128,1152]{1,0:T(8,128)(2,1)S(1)}, bf16[128,1152]{1,0:T(8,128)(2,1)S(1)}, u32[]{:S(2)}, u32[]{:S(2)}) %collective-permute-start.24) | collective-permute-done | bytes 294944 | tf_op jit(solution)/shard_map/ppermute | solution.py:25
  104.2 3.7 %collective-permute-start.25 = (bf16[128,1152]{1,0:T(8,128)(2,1)S(1)}, bf16[128,1152]{1,0:T(8,128)(2,1)S(1)}, u32[]{:S(2)}, u32[]{:S(2)}) collective-permute-start(bf16[128,1152]{1,0:T(8,128)(2,1)S(1)} %add_convert_fusion.4), channel_id=1, source_target_pairs={{0,248},{1,249},{2,250},{3,251},{4,252},{5,253},{6,254},{7,255},{8... | collective-permute-start | bytes 884744 | tf_op jit(solution)/shard_map/ppermute | solution.py:25
  109.0 3.8 %collective-permute-start.29 = (bf16[128,1152]{1,0:T(8,128)(2,1)S(1)}, bf16[128,1152]{1,0:T(8,128)(2,1)S(1)}, u32[]{:S(2)}, u32[]{:S(2)}) collective-permute-start(bf16[128,1152]{1,0:T(8,128)(2,1)S(1)} %add_convert_fusion.2), channel_id=1, source_target_pairs={{0,4},{2,6},{4,0},{6,2},{1,5},{3,7},{5,1},{7,3},{8,12},{10,14},{12... | collective-permute-start | bytes 884744 | tf_op jit(solution)/shard_map/ppermute | solution.py:21
  112.9 3.9 %collective-permute-done.33 = bf16[128,1152]{1,0:T(8,128)(2,1)S(1)} collective-permute-done((bf16[128,1152]{1,0:T(8,128)(2,1)S(1)}, bf16[128,1152]{1,0:T(8,128)(2,1)S(1)}, u32[]{:S(2)}, u32[]{:S(2)}) %collective-permute-start.33) | collective-permute-done | bytes 294944 | tf_op jit(solution)/shard_map/ppermute | solution.py:21
  116.8 2.7 %collective-permute-start.31 = (bf16[128,1152]{1,0:T(8,128)(2,1)S(1)}, bf16[128,1152]{1,0:T(8,128)(2,1)S(1)}, u32[]{:S(2)}, u32[]{:S(2)}) collective-permute-start(bf16[128,1152]{1,0:T(8,128)(2,1)S(1)} %add_convert_fusion.1), channel_id=1, source_target_pairs={{0,6},{2,0},{4,2},{6,4},{1,7},{3,1},{5,3},{7,5},{8,14},{10,8},{12,... | collective-permute-start | bytes 884744 | tf_op jit(solution)/shard_map/ppermute | solution.py:21
  119.6 2.7 %collective-permute-start.34 = (bf16[128,1152]{1,0:T(8,128)(2,1)S(1)}, bf16[128,1152]{1,0:T(8,128)(2,1)S(1)}, u32[]{:S(2)}, u32[]{:S(2)}) collective-permute-start(bf16[128,1152]{1,0:T(8,128)(2,1)S(1)} %collective-permute-done.33), channel_id=1, source_target_pairs={{0,8},{1,9},{2,10},{3,11},{4,12},{5,13},{6,14},{7,15},{8,16},{9,17... | collective-permute-start | bytes 884744 | tf_op jit(solution)/shard_map/ppermute | solution.py:271
  122.5 3.6 %collective-permute-done.29.refs_1_ = bf16[128,1152]{1,0:T(8,128)(2,1)S(1)} collective-permute-done((bf16[128,1152]{1,0:T(8,128)(2,1)S(1)}, bf16[128,1152]{1,0:T(8,128)(2,1)S(1)}, u32[]{:S(2)}, u32[]{:S(2)}) %collective-permute-start.29) | collective-permute-done | bytes 294944 | tf_op jit(solution)/shard_map/ppermute | solution.py:21
  126.2 1.9 %shard_map.65 = f32[128,1152]{1,0:T(8,128)} custom-call(s32[1]{0:T(128)} %bitcast.where_ref, f32[128,1152]{1,0:T(8,128)S(1)} %convert_add_fusion.sum_ref, f32[128,1152]{1,0:T(8,128)S(1)} %copy-done.4, f32[128,128]{1,0:T(8,128)S(1)} %copy-done.6, bf16[1152,1152]{1,0:T(8,128)(2,1)S(1)} %copy-done.2, bf16[128,1152]{1,0:T(8,128)(2,1)S(1)} %collective-permute-done.27.refs_0_, ...), custom_call_target="tpu_custom_call" | custom-call | flops 339738624 | bytes 5373952 | tf_op jit(solution)/shard_map/pallas_call | solution.py:70
  128.9 2.6 %collective-permute-done.32.refs_0_ = bf16[128,1152]{1,0:T(8,128)(2,1)S(1)} collective-permute-done((bf16[128,1152]{1,0:T(8,128)(2,1)S(1)}, bf16[128,1152]{1,0:T(8,128)(2,1)S(1)}, u32[]{:S(2)}, u32[]{:S(2)}) %collective-permute-start.32) | collective-permute-done | bytes 294944 | tf_op jit(solution)/shard_map/ppermute | solution.py:25
  131.5 1.9 %shard_map.66 = f32[128,1152]{1,0:T(8,128)} custom-call(s32[1]{0:T(128)} %bitcast.where_ref, f32[128,1152]{1,0:T(8,128)S(1)} %get-tuple-element.83.sum_ref, f32[128,1152]{1,0:T(8,128)S(1)} %copy-done.3, f32[128,128]{1,0:T(8,128)S(1)} %copy-done.5, bf16[1152,1152]{1,0:T(8,128)(2,1)S(1)} %copy-done.1, bf16[128,1152]{1,0:T(8,128)(2,1)S(1)} %collective-permute-done.32.refs_0_, ...), custom_call_target="tpu_custom_call" | custom-call | flops 339738624 | bytes 5079040 | tf_op jit(solution)/shard_map/pallas_call | solution.py:70
  (104 shorter events, 21.1 us)
Async XLA Ops:
  0.7 14.2 %collective-permute-start.4 = (bf16[128,1152]{1,0:T(8,128)(2,1)}, bf16[128,1152]{1,0:T(8,128)(2,1)S(1)}, u32[]{:S(2)}, u32[]{:S(2)}) collective-permute-start(bf16[128,1152]{1,0:T(8,128)(2,1)} %refs_8_.1), channel_id=1, source_target_pairs={{0,8},{1,9},{2,10},{3,11},{4,12},{5,13},{6,14},{7,15},{8,16},{9,17... | collective-permute-start | bytes 884744 | tf_op jit(solution)/shard_map/ppermute | solution.py:25
  3.7 6.0 %collective-permute-start.3 = (bf16[18,1152]{1,0:T(8,128)(2,1)S(1)}, bf16[18,1152]{1,0:T(8,128)(2,1)S(1)}, u32[]{:S(2)}, u32[]{:S(2)}) collective-permute-start(bf16[18,1152]{1,0:T(8,128)(2,1)S(1)} %pad_maximum_fusion.refs_0_), channel_id=1, source_target_pairs={{0,2},{2,4},{4,6},{6,0},{1,3},{3,5},{5,7},{7,1},{8,10},{10,12},{12... | collective-permute-start | bytes 124424 | tf_op jit(solution)/shard_map/ppermute | solution.py:21
  5.3 6.0 %collective-permute-start.2 = (bf16[18,1152]{1,0:T(8,128)(2,1)S(1)}, bf16[18,1152]{1,0:T(8,128)(2,1)S(1)}, u32[]{:S(2)}, u32[]{:S(2)}) collective-permute-start(bf16[18,1152]{1,0:T(8,128)(2,1)S(1)} %pad_maximum_fusion.refs_0_), channel_id=1, source_target_pairs={{0,4},{2,6},{4,0},{6,2},{1,5},{3,7},{5,1},{7,3},{8,12},{10,14},{12... | collective-permute-start | bytes 124424 | tf_op jit(solution)/shard_map/ppermute | solution.py:21
  8.2 4.2 %collective-permute-start.1 = (bf16[18,1152]{1,0:T(8,128)(2,1)S(1)}, bf16[18,1152]{1,0:T(8,128)(2,1)S(1)}, u32[]{:S(2)}, u32[]{:S(2)}) collective-permute-start(bf16[18,1152]{1,0:T(8,128)(2,1)S(1)} %pad_maximum_fusion.refs_0_), channel_id=1, source_target_pairs={{0,6},{2,0},{4,2},{6,4},{1,7},{3,1},{5,3},{7,5},{8,14},{10,8},{12,... | collective-permute-start | bytes 124424 | tf_op jit(solution)/shard_map/ppermute | solution.py:21
  14.9 20.6 %collective-permute-start.9 = (bf16[128,1280]{1,0:T(8,128)(2,1)S(1)}, bf16[128,1280]{1,0:T(8,128)(2,1)S(1)}, u32[]{:S(2)}, u32[]{:S(2)}) collective-permute-start(bf16[128,1280]{1,0:T(8,128)(2,1)S(1)} %fusion.1.refs_8_), channel_id=1, source_target_pairs={{0,2},{2,4},{4,6},{6,0},{1,3},{3,5},{5,7},{7,1},{8,10},{10,12},{12... | collective-permute-start | bytes 983048 | tf_op jit(solution)/shard_map/ppermute | solution.py:21
  16.5 19.1 %collective-permute-start.8 = (bf16[128,1280]{1,0:T(8,128)(2,1)S(1)}, bf16[128,1280]{1,0:T(8,128)(2,1)S(1)}, u32[]{:S(2)}, u32[]{:S(2)}) collective-permute-start(bf16[128,1280]{1,0:T(8,128)(2,1)S(1)} %fusion.1.refs_8_), channel_id=1, source_target_pairs={{0,4},{2,6},{4,0},{6,2},{1,5},{3,7},{5,1},{7,3},{8,12},{10,14},{12... | collective-permute-start | bytes 983048 | tf_op jit(solution)/shard_map/ppermute | solution.py:21
  19.4 16.2 %collective-permute-start.7 = (bf16[128,1280]{1,0:T(8,128)(2,1)S(1)}, bf16[128,1280]{1,0:T(8,128)(2,1)S(1)}, u32[]{:S(2)}, u32[]{:S(2)}) collective-permute-start(bf16[128,1280]{1,0:T(8,128)(2,1)S(1)} %fusion.1.refs_8_), channel_id=1, source_target_pairs={{0,6},{2,0},{4,2},{6,4},{1,7},{3,1},{5,3},{7,5},{8,14},{10,8},{12,... | collective-permute-start | bytes 983048 | tf_op jit(solution)/shard_map/ppermute | solution.py:21
  20.8 14.8 %collective-permute-start.6 = (bf16[128,1152]{1,0:T(8,128)(2,1)S(1)}, bf16[128,1152]{1,0:T(8,128)(2,1)S(1)}, u32[]{:S(2)}, u32[]{:S(2)}) collective-permute-start(bf16[128,1152]{1,0:T(8,128)(2,1)S(1)} %collective-permute-done.4.refs_9_), channel_id=1, source_target_pairs={{0,8},{1,9},{2,10},{3,11},{4,12},{5,13},{6,14},{7,15},{8,16},{9,17... | collective-permute-start | bytes 884744 | tf_op jit(solution)/shard_map/ppermute | solution.py:25
  20.8 10.9 %collective-permute-start.5 = (bf16[72,1152]{1,0:T(8,128)(2,1)S(1)}, bf16[72,1152]{1,0:T(8,128)(2,1)S(1)}, u32[]{:S(2)}, u32[]{:S(2)}) collective-permute-start(bf16[72,1152]{1,0:T(8,128)(2,1)S(1)} %shard_map.59), channel_id=1, source_target_pairs={{0,232},{1,224},{2,248},{3,208},{4,192},{5,200},{6,240},{7,216},{8... | collective-permute-start | bytes 497672 | tf_op jit(solution)/shard_map/ppermute | solution.py:109
  35.6 11.4 %collective-permute-start.10 = (bf16[128,1152]{1,0:T(8,128)(2,1)S(1)}, bf16[128,1152]{1,0:T(8,128)(2,1)S(1)}, u32[]{:S(2)}, u32[]{:S(2)}) collective-permute-start(bf16[128,1152]{1,0:T(8,128)(2,1)S(1)} %collective-permute-done.6.refs_10_), channel_id=1, source_target_pairs={{0,8},{1,9},{2,10},{3,11},{4,12},{5,13},{6,14},{7,15},{8,16},{9,17... | collective-permute-start | bytes 884744 | tf_op jit(solution)/shard_map/ppermute | solution.py:25
  35.7 6.6 %collective-permute-start.13 = (bf16[72,1152]{1,0:T(8,128)(2,1)S(1)}, bf16[72,1152]{1,0:T(8,128)(2,1)S(1)}, u32[]{:S(2)}, u32[]{:S(2)}) collective-permute-start(bf16[72,1152]{1,0:T(8,128)(2,1)S(1)} %collective-permute-done.5.refs_0_), channel_id=1, source_target_pairs={{6,0},{193,1},{0,2},{195,3},{2,4},{197,5},{4,6},{199,7},{14,8},{20... | collective-permute-start | bytes 497672 | tf_op jit(solution)/shard_map/ppermute | solution.py:44
  35.8 8.7 %collective-permute-start.12 = (bf16[72,1152]{1,0:T(8,128)(2,1)S(1)}, bf16[72,1152]{1,0:T(8,128)(2,1)S(1)}, u32[]{:S(2)}, u32[]{:S(2)}) collective-permute-start(bf16[72,1152]{1,0:T(8,128)(2,1)S(1)} %collective-permute-done.5.refs_0_), channel_id=1, source_target_pairs={{4,0},{129,1},{6,2},{131,3},{0,4},{133,5},{2,6},{135,7},{12,8},{13... | collective-permute-start | bytes 497672 | tf_op jit(solution)/shard_map/ppermute | solution.py:44
  39.4 5.6 %collective-permute-start.11 = (bf16[72,1152]{1,0:T(8,128)(2,1)S(1)}, bf16[72,1152]{1,0:T(8,128)(2,1)S(1)}, u32[]{:S(2)}, u32[]{:S(2)}) collective-permute-start(bf16[72,1152]{1,0:T(8,128)(2,1)S(1)} %collective-permute-done.5.refs_0_), channel_id=1, source_target_pairs={{2,0},{65,1},{4,2},{67,3},{6,4},{69,5},{0,6},{71,7},{10,8},{73,9},... | collective-permute-start | bytes 497672 | tf_op jit(solution)/shard_map/ppermute | solution.py:44
  47.7 19.6 %collective-permute-start.18 = (bf16[288,1152]{1,0:T(8,128)(2,1)S(1)}, bf16[288,1152]{1,0:T(8,128)(2,1)S(1)}, u32[]{:S(2)}, u32[]{:S(2)}) collective-permute-start(bf16[288,1152]{1,0:T(8,128)(2,1)S(1)} %shard_map.60.refs_0_), channel_id=1, source_target_pairs={{192,0},{7,1},{194,2},{1,3},{196,4},{3,5},{198,6},{5,7},{200,8},{1... | collective-permute-start | bytes 1990664 | tf_op jit(solution)/shard_map/ppermute | solution.py:44
  49.1 24.3 %collective-permute-start.17 = (bf16[288,1152]{1,0:T(8,128)(2,1)S(1)}, bf16[288,1152]{1,0:T(8,128)(2,1)S(1)}, u32[]{:S(2)}, u32[]{:S(2)}) collective-permute-start(bf16[288,1152]{1,0:T(8,128)(2,1)S(1)} %shard_map.60.refs_0_), channel_id=1, source_target_pairs={{128,0},{5,1},{130,2},{7,3},{132,4},{1,5},{134,6},{3,7},{136,8},{1... | collective-permute-start | bytes 1990664 | tf_op jit(solution)/shard_map/ppermute | solution.py:44
  50.2 23.2 %collective-permute-start.16 = (bf16[288,1152]{1,0:T(8,128)(2,1)S(1)}, bf16[288,1152]{1,0:T(8,128)(2,1)S(1)}, u32[]{:S(2)}, u32[]{:S(2)}) collective-permute-start(bf16[288,1152]{1,0:T(8,128)(2,1)S(1)} %shard_map.60.refs_0_), channel_id=1, source_target_pairs={{64,0},{3,1},{66,2},{5,3},{68,4},{7,5},{70,6},{1,7},{72,8},{11,9},... | collective-permute-start | bytes 1990664 | tf_op jit(solution)/shard_map/ppermute | solution.py:44
  51.7 21.6 %collective-permute-start.15 = (bf16[288,1152]{1,0:T(8,128)(2,1)S(1)}, bf16[288,1152]{1,0:T(8,128)(2,1)S(1)}, u32[]{:S(2)}, u32[]{:S(2)}) collective-permute-start(bf16[288,1152]{1,0:T(8,128)(2,1)S(1)} %shard_map.60.refs_0_), channel_id=1, source_target_pairs={{0,1},{1,0},{2,3},{3,2},{4,5},{5,4},{6,7},{7,6},{8,9},{9,8},{10,11... | collective-permute-start | bytes 1990664 | tf_op jit(solution)/shard_map/ppermute | solution.py:21
  53.8 13.5 %collective-permute-start.14 = (bf16[128,1152]{1,0:T(8,128)(2,1)}, bf16[128,1152]{1,0:T(8,128)(2,1)S(1)}, u32[]{:S(2)}, u32[]{:S(2)}) collective-permute-start(bf16[128,1152]{1,0:T(8,128)(2,1)} %copy-done.20), channel_id=1, source_target_pairs={{0,8},{1,9},{2,10},{3,11},{4,12},{5,13},{6,14},{7,15},{8,16},{9,17... | collective-permute-start | bytes 884744 | tf_op jit(solution)/shard_map/ppermute | solution.py:25
  73.5 3.2 %collective-permute-start.20 = (bf16[288,1152]{1,0:T(8,128)(2,1)S(1)}, bf16[288,1152]{1,0:T(8,128)(2,1)}, u32[]{:S(2)}, u32[]{:S(2)}) collective-permute-start(bf16[288,1152]{1,0:T(8,128)(2,1)S(1)} %collective-permute-done.17.refs_2_), channel_id=1, source_target_pairs={{0,1},{1,0},{2,3},{3,2},{4,5},{5,4},{6,7},{7,6},{8,9},{9,8},{10,11... | collective-permute-start | bytes 1990664 | tf_op jit(solution)/shard_map/ppermute | solution.py:21
  74.0 3.6 %collective-permute-start.21 = (bf16[288,1152]{1,0:T(8,128)(2,1)S(1)}, bf16[288,1152]{1,0:T(8,128)(2,1)}, u32[]{:S(2)}, u32[]{:S(2)}) collective-permute-start(bf16[288,1152]{1,0:T(8,128)(2,1)S(1)} %collective-permute-done.18.refs_3_), channel_id=1, source_target_pairs={{0,1},{1,0},{2,3},{3,2},{4,5},{5,4},{6,7},{7,6},{8,9},{9,8},{10,11... | collective-permute-start | bytes 1990664 | tf_op jit(solution)/shard_map/ppermute | solution.py:21
  83.8 7.1 %collective-permute-start.22 = (bf16[512,1280]{1,0:T(8,128)(2,1)}, bf16[512,1280]{1,0:T(8,128)(2,1)S(1)}, u32[]{:S(2)}, u32[]{:S(2)}) collective-permute-start(bf16[512,1280]{1,0:T(8,128)(2,1)} %get-tuple-element.64.own_emb), channel_id=1, source_target_pairs={{0,1},{1,0},{2,3},{3,2},{4,5},{5,4},{6,7},{7,6},{8,9},{9,8},{10,11... | collective-permute-start | bytes 3932168 | tf_op jit(solution)/shard_map/ppermute | solution.py:21
  94.7 9.4 %collective-permute-start.24 = (bf16[128,1152]{1,0:T(8,128)(2,1)S(1)}, bf16[128,1152]{1,0:T(8,128)(2,1)S(1)}, u32[]{:S(2)}, u32[]{:S(2)}) collective-permute-start(bf16[128,1152]{1,0:T(8,128)(2,1)S(1)} %get-tuple-element.74), channel_id=1, source_target_pairs={{0,248},{1,249},{2,250},{3,251},{4,252},{5,253},{6,254},{7,255},{8... | collective-permute-start | bytes 884744 | tf_op jit(solution)/shard_map/ppermute | solution.py:25
  94.8 22.0 %collective-permute-start.33 = (bf16[128,1152]{1,0:T(8,128)(2,1)S(1)}, bf16[128,1152]{1,0:T(8,128)(2,1)S(1)}, u32[]{:S(2)}, u32[]{:S(2)}) collective-permute-start(bf16[128,1152]{1,0:T(8,128)(2,1)S(1)} %get-tuple-element.89), channel_id=1, source_target_pairs={{0,24},{8,32},{16,40},{24,48},{32,56},{40,0},{48,8},{56,16},{1,25}... | collective-permute-start | bytes 884744 | tf_op jit(solution)/shard_map/ppermute | solution.py:21
  100.7 21.7 %collective-permute-start.23 = (bf16[128,1152]{1,0:T(8,128)(2,1)S(1)}, bf16[128,1152]{1,0:T(8,128)(2,1)S(1)}, u32[]{:S(2)}, u32[]{:S(2)}) collective-permute-start(bf16[128,1152]{1,0:T(8,128)(2,1)S(1)} %get-tuple-element.70), channel_id=1, source_target_pairs={{0,1},{1,0},{2,3},{3,2},{4,5},{5,4},{6,7},{7,6},{8,9},{9,8},{10,11... | collective-permute-start | bytes 884744 | tf_op jit(solution)/shard_map/ppermute | solution.py:21
  101.3 6.6 %collective-permute-start.28 = (bf16[128,1152]{1,0:T(8,128)(2,1)S(1)}, bf16[128,1152]{1,0:T(8,128)(2,1)S(1)}, u32[]{:S(2)}, u32[]{:S(2)}) collective-permute-start(bf16[128,1152]{1,0:T(8,128)(2,1)S(1)} %get-tuple-element.80), channel_id=1, source_target_pairs={{0,1},{1,0},{2,3},{3,2},{4,5},{5,4},{6,7},{7,6},{8,9},{9,8},{10,11... | collective-permute-start | bytes 884744 | tf_op jit(solution)/shard_map/ppermute | solution.py:21
  104.1 4.9 %collective-permute-start.30 = (bf16[128,1152]{1,0:T(8,128)(2,1)S(1)}, bf16[128,1152]{1,0:T(8,128)(2,1)S(1)}, u32[]{:S(2)}, u32[]{:S(2)}) collective-permute-start(bf16[128,1152]{1,0:T(8,128)(2,1)S(1)} %get-tuple-element.82), channel_id=1, source_target_pairs={{0,1},{1,0},{2,3},{3,2},{4,5},{5,4},{6,7},{7,6},{8,9},{9,8},{10,11... | collective-permute-start | bytes 884744 | tf_op jit(solution)/shard_map/ppermute | solution.py:21
  104.2 15.4 %collective-permute-start.25 = (bf16[128,1152]{1,0:T(8,128)(2,1)S(1)}, bf16[128,1152]{1,0:T(8,128)(2,1)S(1)}, u32[]{:S(2)}, u32[]{:S(2)}) collective-permute-start(bf16[128,1152]{1,0:T(8,128)(2,1)S(1)} %add_convert_fusion.4), channel_id=1, source_target_pairs={{0,248},{1,249},{2,250},{3,251},{4,252},{5,253},{6,254},{7,255},{8... | collective-permute-start | bytes 884744 | tf_op jit(solution)/shard_map/ppermute | solution.py:25
  107.9 14.4 %collective-permute-start.27 = (bf16[128,1152]{1,0:T(8,128)(2,1)S(1)}, bf16[128,1152]{1,0:T(8,128)(2,1)S(1)}, u32[]{:S(2)}, u32[]{:S(2)}) collective-permute-start(bf16[128,1152]{1,0:T(8,128)(2,1)S(1)} %add_convert_fusion.3), channel_id=1, source_target_pairs={{0,2},{2,4},{4,6},{6,0},{1,3},{3,5},{5,7},{7,1},{8,10},{10,12},{12... | collective-permute-start | bytes 884744 | tf_op jit(solution)/shard_map/ppermute | solution.py:21
  109.0 17.1 %collective-permute-start.29 = (bf16[128,1152]{1,0:T(8,128)(2,1)S(1)}, bf16[128,1152]{1,0:T(8,128)(2,1)S(1)}, u32[]{:S(2)}, u32[]{:S(2)}) collective-permute-start(bf16[128,1152]{1,0:T(8,128)(2,1)S(1)} %add_convert_fusion.2), channel_id=1, source_target_pairs={{0,4},{2,6},{4,0},{6,2},{1,5},{3,7},{5,1},{7,3},{8,12},{10,14},{12... | collective-permute-start | bytes 884744 | tf_op jit(solution)/shard_map/ppermute | solution.py:21
  116.8 9.3 %collective-permute-start.31 = (bf16[128,1152]{1,0:T(8,128)(2,1)S(1)}, bf16[128,1152]{1,0:T(8,128)(2,1)S(1)}, u32[]{:S(2)}, u32[]{:S(2)}) collective-permute-start(bf16[128,1152]{1,0:T(8,128)(2,1)S(1)} %add_convert_fusion.1), channel_id=1, source_target_pairs={{0,6},{2,0},{4,2},{6,4},{1,7},{3,1},{5,3},{7,5},{8,14},{10,8},{12,... | collective-permute-start | bytes 884744 | tf_op jit(solution)/shard_map/ppermute | solution.py:21
  119.6 9.3 %collective-permute-start.34 = (bf16[128,1152]{1,0:T(8,128)(2,1)S(1)}, bf16[128,1152]{1,0:T(8,128)(2,1)S(1)}, u32[]{:S(2)}, u32[]{:S(2)}) collective-permute-start(bf16[128,1152]{1,0:T(8,128)(2,1)S(1)} %collective-permute-done.33), channel_id=1, source_target_pairs={{0,8},{1,9},{2,10},{3,11},{4,12},{5,13},{6,14},{7,15},{8,16},{9,17... | collective-permute-start | bytes 884744 | tf_op jit(solution)/shard_map/ppermute | solution.py:271
  122.4 9.2 %collective-permute-start.32 = (bf16[128,1152]{1,0:T(8,128)(2,1)S(1)}, bf16[128,1152]{1,0:T(8,128)(2,1)S(1)}, u32[]{:S(2)}, u32[]{:S(2)}) collective-permute-start(bf16[128,1152]{1,0:T(8,128)(2,1)S(1)} %add_convert_fusion), channel_id=1, source_target_pairs={{0,248},{1,249},{2,250},{3,251},{4,252},{5,253},{6,254},{7,255},{8... | collective-permute-start | bytes 884744 | tf_op jit(solution)/shard_map/ppermute | solution.py:25
  (25 other events, 222.2 us)

commit v2 on v1

--- a/solution.py
+++ b/solution.py
@@ -342,6 +342,7 @@
     home = last_step_home(home)
     second, arrived[0] = tied((second, arrived[0]))
     first = blocks_behind((second.astype(jnp.float32) + text_sums[1]).astype(low), -8)
+    first, arrived[1] = tied((first, arrived[1]))
     flops = 2 * rows * width * width
     (image_grad,) = on_device(finish, (y,), [chip[0], image_unit, image_norm, image_weight, *arrived], [wide], flops=flops, vmem=16)
     (text_grad,) = on_device(finish, (y,), [text_sums[0], text_unit, text_norm, text_weight, first, home], [wide], flops=flops, vmem=16)

time: 134 us -> 136 us (1.015)
  waiting for transfers between devices: 55.7 us -> 57.6 us
    ppermute x7, waiting for transfers between devices: 26.2 us -> 29 us  [blocks_behind(): lax.ppermute(value, AXES, [(i, (i + steps) % 256) for i in range(256)])]
  transfers between devices with their start and end apart: 35 -> 35, of which waited for: 20 -> 19; matrix products, arithmetic and copies ran while one was open for 3% -> 3% of each run, Pallas kernels for 11% -> 11%
where the time goes in v2:
time: 136 us; the launch traced here: 135 us
  waiting for transfers between devices  57.6 us (42%)
  starting transfers between devices  45.4 us (33%)
  Pallas kernels  25.6 us (19%)
  other arithmetic  3.66 us (3%)
  local copies, waits for them, and re-layouts  2.12 us (2%)
    ppermute x7, waiting for transfers between devices, blocks_behind(): lax.ppermute(value, AXES, [(i, (i + steps) % 256) for i in range(256)])  29 us
    pallas_call x8, Pallas kernels, on_device(): pl.pallas_call(body, out_shape=outs, in_specs=[pl.BlockSpec(memory_space=...  25.6 us
    ppermute x20, starting transfers between devices, along(): lax.ppermute(value, axis, [(i, (i + steps) % count) for i in range(count)])  23.7 us
    ppermute x20, waiting for transfers between devices, along(): lax.ppermute(value, axis, [(i, (i + steps) % count) for i in range(count)])  13.2 us
    ppermute x6, waiting for transfers between devices, crosswise(): return lax.ppermute(value, AXES, pairs)  10.1 us
    ppermute x6, starting transfers between devices, crosswise(): return lax.ppermute(value, AXES, pairs)  9.16 us
    ppermute x1, starting transfers between devices, spread_units(): return lax.ppermute(unit, AXES, pairs)  5.63 us
    ppermute x1, waiting for transfers between devices, spread_units(): return lax.ppermute(unit, AXES, pairs)  5.28 us
  transfers between devices with their start and end apart: 35, of which 19 were waited for; matrix products, arithmetic and copies ran while one was open for 3% of the time, Pallas kernels for 11%

profile of v2, /device:TPU:0, one launch (start us, length us, event | category | flops | bytes accessed | tf_op | source)
XLA Modules:
  0.0 135.3 jit_solution(2460688807685692368)
XLA Ops:
  3.7 1.7 %collective-permute-start.3 = (bf16[18,1152]{1,0:T(8,128)(2,1)S(1)}, bf16[18,1152]{1,0:T(8,128)(2,1)S(1)}, u32[]{:S(2)}, u32[]{:S(2)}) collective-permute-start(bf16[18,1152]{1,0:T(8,128)(2,1)S(1)} %pad_maximum_fusion.refs_0_), channel_id=1, source_target_pairs={{0,2},{2,4},{4,6},{6,0},{1,3},{3,5},{5,7},{7,1},{8,10},{10,12},{12... | collective-permute-start | bytes 124424 | tf_op jit(solution)/shard_map/ppermute | solution.py:21
  5.3 2.9 %collective-permute-start.2 = (bf16[18,1152]{1,0:T(8,128)(2,1)S(1)}, bf16[18,1152]{1,0:T(8,128)(2,1)S(1)}, u32[]{:S(2)}, u32[]{:S(2)}) collective-permute-start(bf16[18,1152]{1,0:T(8,128)(2,1)S(1)} %pad_maximum_fusion.refs_0_), channel_id=1, source_target_pairs={{0,4},{2,6},{4,0},{6,2},{1,5},{3,7},{5,1},{7,3},{8,12},{10,14},{12... | collective-permute-start | bytes 124424 | tf_op jit(solution)/shard_map/ppermute | solution.py:21
  9.7 1.7 %collective-permute-done.2.refs_2_ = bf16[18,1152]{1,0:T(8,128)(2,1)S(1)} collective-permute-done((bf16[18,1152]{1,0:T(8,128)(2,1)S(1)}, bf16[18,1152]{1,0:T(8,128)(2,1)S(1)}, u32[]{:S(2)}, u32[]{:S(2)}) %collective-permute-start.2) | collective-permute-done | bytes 41504 | tf_op jit(solution)/shard_map/ppermute | solution.py:21
  13.1 1.8 %collective-permute-done.4.refs_9_ = bf16[128,1152]{1,0:T(8,128)(2,1)S(1)} collective-permute-done((bf16[128,1152]{1,0:T(8,128)(2,1)}, bf16[128,1152]{1,0:T(8,128)(2,1)S(1)}, u32[]{:S(2)}, u32[]{:S(2)}) %collective-permute-start.4) | collective-permute-done | bytes 294944 | tf_op jit(solution)/shard_map/ppermute | solution.py:25
  14.9 1.6 %collective-permute-start.9 = (bf16[128,1280]{1,0:T(8,128)(2,1)S(1)}, bf16[128,1280]{1,0:T(8,128)(2,1)S(1)}, u32[]{:S(2)}, u32[]{:S(2)}) collective-permute-start(bf16[128,1280]{1,0:T(8,128)(2,1)S(1)} %fusion.1.refs_8_), channel_id=1, source_target_pairs={{0,2},{2,4},{4,6},{6,0},{1,3},{3,5},{5,7},{7,1},{8,10},{10,12},{12... | collective-permute-start | bytes 983048 | tf_op jit(solution)/shard_map/ppermute | solution.py:21
  16.5 2.9 %collective-permute-start.8 = (bf16[128,1280]{1,0:T(8,128)(2,1)S(1)}, bf16[128,1280]{1,0:T(8,128)(2,1)S(1)}, u32[]{:S(2)}, u32[]{:S(2)}) collective-permute-start(bf16[128,1280]{1,0:T(8,128)(2,1)S(1)} %fusion.1.refs_8_), channel_id=1, source_target_pairs={{0,4},{2,6},{4,0},{6,2},{1,5},{3,7},{5,1},{7,3},{8,12},{10,14},{12... | collective-permute-start | bytes 983048 | tf_op jit(solution)/shard_map/ppermute | solution.py:21
  20.8 5.6 %collective-permute-start.5 = (bf16[72,1152]{1,0:T(8,128)(2,1)S(1)}, bf16[72,1152]{1,0:T(8,128)(2,1)S(1)}, u32[]{:S(2)}, u32[]{:S(2)}) collective-permute-start(bf16[72,1152]{1,0:T(8,128)(2,1)S(1)} %shard_map.59), channel_id=1, source_target_pairs={{0,232},{1,224},{2,248},{3,208},{4,192},{5,200},{6,240},{7,216},{8... | collective-permute-start | bytes 497672 | tf_op jit(solution)/shard_map/ppermute | solution.py:109
  26.4 5.3 %collective-permute-done.5.refs_0_ = bf16[72,1152]{1,0:T(8,128)(2,1)S(1)} collective-permute-done((bf16[72,1152]{1,0:T(8,128)(2,1)S(1)}, bf16[72,1152]{1,0:T(8,128)(2,1)S(1)}, u32[]{:S(2)}, u32[]{:S(2)}) %collective-permute-start.5) | collective-permute-done | bytes 165920 | tf_op jit(solution)/shard_map/ppermute | solution.py:109
  31.7 3.9 %collective-permute-done.6.refs_10_ = bf16[128,1152]{1,0:T(8,128)(2,1)S(1)} collective-permute-done((bf16[128,1152]{1,0:T(8,128)(2,1)S(1)}, bf16[128,1152]{1,0:T(8,128)(2,1)S(1)}, u32[]{:S(2)}, u32[]{:S(2)}) %collective-permute-start.6) | collective-permute-done | bytes 294944 | tf_op jit(solution)/shard_map/ppermute | solution.py:25
  35.8 3.6 %collective-permute-start.12 = (bf16[72,1152]{1,0:T(8,128)(2,1)S(1)}, bf16[72,1152]{1,0:T(8,128)(2,1)S(1)}, u32[]{:S(2)}, u32[]{:S(2)}) collective-permute-start(bf16[72,1152]{1,0:T(8,128)(2,1)S(1)} %collective-permute-done.5.refs_0_), channel_id=1, source_target_pairs={{4,0},{129,1},{6,2},{131,3},{0,4},{133,5},{2,6},{135,7},{12,8},{13... | collective-permute-start | bytes 497672 | tf_op jit(solution)/shard_map/ppermute | solution.py:44
  39.4 1.5 %collective-permute-start.11 = (bf16[72,1152]{1,0:T(8,128)(2,1)S(1)}, bf16[72,1152]{1,0:T(8,128)(2,1)S(1)}, u32[]{:S(2)}, u32[]{:S(2)}) collective-permute-start(bf16[72,1152]{1,0:T(8,128)(2,1)S(1)} %collective-permute-done.5.refs_0_), channel_id=1, source_target_pairs={{2,0},{65,1},{4,2},{67,3},{6,4},{69,5},{0,6},{71,7},{10,8},{73,9},... | collective-permute-start | bytes 497672 | tf_op jit(solution)/shard_map/ppermute | solution.py:44
  40.9 1.4 %collective-permute-done.13.refs_3_ = bf16[72,1152]{1,0:T(8,128)(2,1)S(1)} collective-permute-done((bf16[72,1152]{1,0:T(8,128)(2,1)S(1)}, bf16[72,1152]{1,0:T(8,128)(2,1)S(1)}, u32[]{:S(2)}, u32[]{:S(2)}) %collective-permute-start.13) | collective-permute-done | bytes 165920 | tf_op jit(solution)/shard_map/ppermute | solution.py:44
  42.4 2.1 %collective-permute-done.12.refs_2_ = bf16[72,1152]{1,0:T(8,128)(2,1)S(1)} collective-permute-done((bf16[72,1152]{1,0:T(8,128)(2,1)S(1)}, bf16[72,1152]{1,0:T(8,128)(2,1)S(1)}, u32[]{:S(2)}, u32[]{:S(2)}) %collective-permute-start.12) | collective-permute-done | bytes 165920 | tf_op jit(solution)/shard_map/ppermute | solution.py:44
  45.0 2.0 %collective-permute-done.10.refs_11_ = bf16[128,1152]{1,0:T(8,128)(2,1)S(1)} collective-permute-done((bf16[128,1152]{1,0:T(8,128)(2,1)S(1)}, bf16[128,1152]{1,0:T(8,128)(2,1)S(1)}, u32[]{:S(2)}, u32[]{:S(2)}) %collective-permute-start.10) | collective-permute-done | bytes 294944 | tf_op jit(solution)/shard_map/ppermute | solution.py:25
  50.2 1.5 %collective-permute-start.16 = (bf16[288,1152]{1,0:T(8,128)(2,1)S(1)}, bf16[288,1152]{1,0:T(8,128)(2,1)S(1)}, u32[]{:S(2)}, u32[]{:S(2)}) collective-permute-start(bf16[288,1152]{1,0:T(8,128)(2,1)S(1)} %shard_map.60.refs_0_), channel_id=1, source_target_pairs={{64,0},{3,1},{66,2},{5,3},{68,4},{7,5},{70,6},{1,7},{72,8},{11,9},... | collective-permute-start | bytes 1990664 | tf_op jit(solution)/shard_map/ppermute | solution.py:44
  51.7 2.1 %collective-permute-start.15 = (bf16[288,1152]{1,0:T(8,128)(2,1)S(1)}, bf16[288,1152]{1,0:T(8,128)(2,1)S(1)}, u32[]{:S(2)}, u32[]{:S(2)}) collective-permute-start(bf16[288,1152]{1,0:T(8,128)(2,1)S(1)} %shard_map.60.refs_0_), channel_id=1, source_target_pairs={{0,1},{1,0},{2,3},{3,2},{4,5},{5,4},{6,7},{7,6},{8,9},{9,8},{10,11... | collective-permute-start | bytes 1990664 | tf_op jit(solution)/shard_map/ppermute | solution.py:21
  53.8 13.5 %collective-permute-done.14.refs_12_ = bf16[128,1152]{1,0:T(8,128)(2,1)S(1)} collective-permute-done((bf16[128,1152]{1,0:T(8,128)(2,1)}, bf16[128,1152]{1,0:T(8,128)(2,1)S(1)}, u32[]{:S(2)}, u32[]{:S(2)}) %collective-permute-start.14) | collective-permute-done | bytes 294944 | tf_op jit(solution)/shard_map/ppermute | solution.py:25
  67.3 6.0 %collective-permute-done.17.refs_2_ = bf16[288,1152]{1,0:T(8,128)(2,1)S(1)} collective-permute-done((bf16[288,1152]{1,0:T(8,128)(2,1)S(1)}, bf16[288,1152]{1,0:T(8,128)(2,1)S(1)}, u32[]{:S(2)}, u32[]{:S(2)}) %collective-permute-start.17) | collective-permute-done | bytes 663584 | tf_op jit(solution)/shard_map/ppermute | solution.py:44
  77.6 6.1 %shard_map.61 = (bf16[1152,1152]{1,0:T(8,128)(2,1)}, bf16[512,1280]{1,0:T(8,128)(2,1)}, f32[128,1152]{1,0:T(8,128)}, f32[128,128]{1,0:T(8,128)}) custom-call(s32[4]{0:T(128)} %pad_add_fusion.1.where_ref, bf16[288,1152]{1,0:T(8,128)(2,1)} %copy-done, bf16[288,1152]{1,0:T(8,128)(2,1)} %copy-done.12, bf16[288,1152]{1,0:T(8,128)(2,1)} %copy-done.11, ...), custom_call_target="tpu_custom_call" | custom-call | flops 1358954496 | bytes 11239424 | tf_op jit(solution)/shard_map/pallas_call | solution.py:70
  84.1 6.8 %shard_map.62 = (bf16[1152,1152]{1,0:T(8,128)(2,1)}, bf16[640,1152]{1,0:T(8,128)(2,1)}, f32[128,1152]{1,0:T(8,128)}, f32[128,128]{1,0:T(8,128)}) custom-call(s32[4]{0:T(128)} %pad_add_fusion.1.where_ref, bf16[288,1152]{1,0:T(8,128)(2,1)} %copy-done, bf16[288,1152]{1,0:T(8,128)(2,1)} %copy-done.12, bf16[288,1152]{1,0:T(8,128)(2,1)} %copy-done.11, ...), custom_call_target="tpu_custom_call" | custom-call | flops 1698693120 | bytes 11567104 | tf_op jit(solution)/shard_map/pallas_call | solution.py:70
  92.2 2.4 %shard_map.63 = (bf16[512,256]{1,0:T(8,128)(2,1)S(1)}, bf16[512,256]{1,0:T(8,128)(2,1)S(1)}, bf16[128,1152]{1,0:T(8,128)(2,1)S(1)}, bf16[128,1152]{1,0:T(8,128)(2,1)S(1)}) custom-call(s32[2]{0:T(128)S(1)} %pad_add_fusion.where_ref, bf16[512,1280]{1,0:T(8,128)(2,1)S(1)} %copy-done.9, bf16[512,1280]{1,0:T(8,128)(2,1)S(1)} %collective-permute-done.22.other_emb, ...), custom_call_target="tpu_custom_call" | custom-call | flops 1207959552 | bytes 5210112 | tf_op jit(solution)/shard_map/pallas_call | solution.py:70
  95.1 5.6 %shard_map.64 = (f32[128,1152]{1,0:T(8,128)S(1)}, f32[128,1152]{1,0:T(8,128)S(1)}, f32[128,1152]{1,0:T(8,128)S(1)}, f32[128,1152]{1,0:T(8,128)S(1)}, f32[128,115...) custom-call(s32[2]{0:T(128)S(1)} %pad_add_fusion.where_ref, ...), custom_call_target="tpu_custom_call" | custom-call | flops 3321888768 | bytes 9928704 | tf_op jit(solution)/shard_map/pallas_call | solution.py:70
  101.7 2.4 %collective-permute-done.24 = bf16[128,1152]{1,0:T(8,128)(2,1)S(1)} collective-permute-done((bf16[128,1152]{1,0:T(8,128)(2,1)S(1)}, bf16[128,1152]{1,0:T(8,128)(2,1)S(1)}, u32[]{:S(2)}, u32[]{:S(2)}) %collective-permute-start.24) | collective-permute-done | bytes 294944 | tf_op jit(solution)/shard_map/ppermute | solution.py:25
  104.1 3.7 %collective-permute-start.25 = (bf16[128,1152]{1,0:T(8,128)(2,1)S(1)}, bf16[128,1152]{1,0:T(8,128)(2,1)S(1)}, u32[]{:S(2)}, u32[]{:S(2)}) collective-permute-start(bf16[128,1152]{1,0:T(8,128)(2,1)S(1)} %add_convert_fusion.4), channel_id=1, source_target_pairs={{0,248},{1,249},{2,250},{3,251},{4,252},{5,253},{6,254},{7,255},{8... | collective-permute-start | bytes 884744 | tf_op jit(solution)/shard_map/ppermute | solution.py:25
  109.0 3.8 %collective-permute-start.30 = (bf16[128,1152]{1,0:T(8,128)(2,1)S(1)}, bf16[128,1152]{1,0:T(8,128)(2,1)S(1)}, u32[]{:S(2)}, u32[]{:S(2)}) collective-permute-start(bf16[128,1152]{1,0:T(8,128)(2,1)S(1)} %add_convert_fusion.1), channel_id=1, source_target_pairs={{0,4},{2,6},{4,0},{6,2},{1,5},{3,7},{5,1},{7,3},{8,12},{10,14},{12... | collective-permute-start | bytes 884744 | tf_op jit(solution)/shard_map/ppermute | solution.py:21
  112.9 3.9 %collective-permute-done.33 = bf16[128,1152]{1,0:T(8,128)(2,1)S(1)} collective-permute-done((bf16[128,1152]{1,0:T(8,128)(2,1)S(1)}, bf16[128,1152]{1,0:T(8,128)(2,1)S(1)}, u32[]{:S(2)}, u32[]{:S(2)}) %collective-permute-start.33) | collective-permute-done | bytes 294944 | tf_op jit(solution)/shard_map/ppermute | solution.py:21
  116.8 2.7 %collective-permute-start.32 = (bf16[128,1152]{1,0:T(8,128)(2,1)S(1)}, bf16[128,1152]{1,0:T(8,128)(2,1)S(1)}, u32[]{:S(2)}, u32[]{:S(2)}) collective-permute-start(bf16[128,1152]{1,0:T(8,128)(2,1)S(1)} %add_convert_fusion), channel_id=1, source_target_pairs={{0,6},{2,0},{4,2},{6,4},{1,7},{3,1},{5,3},{7,5},{8,14},{10,8},{12,... | collective-permute-start | bytes 884744 | tf_op jit(solution)/shard_map/ppermute | solution.py:21
  119.5 2.7 %collective-permute-start.34 = (bf16[128,1152]{1,0:T(8,128)(2,1)S(1)}, bf16[128,1152]{1,0:T(8,128)(2,1)S(1)}, u32[]{:S(2)}, u32[]{:S(2)}) collective-permute-start(bf16[128,1152]{1,0:T(8,128)(2,1)S(1)} %collective-permute-done.33), channel_id=1, source_target_pairs={{0,8},{1,9},{2,10},{3,11},{4,12},{5,13},{6,14},{7,15},{8,16},{9,17... | collective-permute-start | bytes 884744 | tf_op jit(solution)/shard_map/ppermute | solution.py:271
  122.5 3.6 %collective-permute-done.30.refs_1_ = bf16[128,1152]{1,0:T(8,128)(2,1)S(1)} collective-permute-done((bf16[128,1152]{1,0:T(8,128)(2,1)S(1)}, bf16[128,1152]{1,0:T(8,128)(2,1)S(1)}, u32[]{:S(2)}, u32[]{:S(2)}) %collective-permute-start.30) | collective-permute-done | bytes 294944 | tf_op jit(solution)/shard_map/ppermute | solution.py:21
  126.1 5.4 %collective-permute-done.28.refs_0_ = bf16[128,1152]{1,0:T(8,128)(2,1)S(1)} collective-permute-done((bf16[128,1152]{1,0:T(8,128)(2,1)S(1)}, bf16[128,1152]{1,0:T(8,128)(2,1)S(1)}, u32[]{:S(2)}, u32[]{:S(2)}) %collective-permute-start.28) | collective-permute-done | bytes 294944 | tf_op jit(solution)/shard_map/ppermute | solution.py:25
  131.5 1.9 %shard_map.66 = f32[128,1152]{1,0:T(8,128)} custom-call(s32[1]{0:T(128)} %bitcast.where_ref, f32[128,1152]{1,0:T(8,128)S(1)} %get-tuple-element.88.sum_ref, f32[128,1152]{1,0:T(8,128)S(1)} %copy-done.4, f32[128,128]{1,0:T(8,128)S(1)} %copy-done.6, bf16[1152,1152]{1,0:T(8,128)(2,1)S(1)} %copy-done.1, bf16[128,1152]{1,0:T(8,128)(2,1)S(1)} %collective-permute-done.28.refs_0_, ...), custom_call_target="tpu_custom_call" | custom-call | flops 339738624 | bytes 5079040 | tf_op jit(solution)/shard_map/pallas_call | solution.py:70
  133.4 1.9 %shard_map.65 = f32[128,1152]{1,0:T(8,128)} custom-call(s32[1]{0:T(128)} %bitcast.where_ref, f32[128,1152]{1,0:T(8,128)S(1)} %convert_add_fusion.sum_ref, f32[128,1152]{1,0:T(8,128)S(1)} %copy-done.3, f32[128,128]{1,0:T(8,128)S(1)} %copy-done.5, bf16[1152,1152]{1,0:T(8,128)(2,1)S(1)} %copy-done.2, bf16[128,1152]{1,0:T(8,128)(2,1)S(1)} %collective-permute-done.27.refs_0_, ...), custom_call_target="tpu_custom_call" | custom-call | flops 339738624 | bytes 5373952 | tf_op jit(solution)/shard_map/pallas_call | solution.py:70
  (104 shorter events, 20.3 us)
Async XLA Ops:
  0.7 14.2 %collective-permute-start.4 = (bf16[128,1152]{1,0:T(8,128)(2,1)}, bf16[128,1152]{1,0:T(8,128)(2,1)S(1)}, u32[]{:S(2)}, u32[]{:S(2)}) collective-permute-start(bf16[128,1152]{1,0:T(8,128)(2,1)} %refs_8_.1), channel_id=1, source_target_pairs={{0,8},{1,9},{2,10},{3,11},{4,12},{5,13},{6,14},{7,15},{8,16},{9,17... | collective-permute-start | bytes 884744 | tf_op jit(solution)/shard_map/ppermute | solution.py:25
  3.7 6.0 %collective-permute-start.3 = (bf16[18,1152]{1,0:T(8,128)(2,1)S(1)}, bf16[18,1152]{1,0:T(8,128)(2,1)S(1)}, u32[]{:S(2)}, u32[]{:S(2)}) collective-permute-start(bf16[18,1152]{1,0:T(8,128)(2,1)S(1)} %pad_maximum_fusion.refs_0_), channel_id=1, source_target_pairs={{0,2},{2,4},{4,6},{6,0},{1,3},{3,5},{5,7},{7,1},{8,10},{10,12},{12... | collective-permute-start | bytes 124424 | tf_op jit(solution)/shard_map/ppermute | solution.py:21
  5.3 6.0 %collective-permute-start.2 = (bf16[18,1152]{1,0:T(8,128)(2,1)S(1)}, bf16[18,1152]{1,0:T(8,128)(2,1)S(1)}, u32[]{:S(2)}, u32[]{:S(2)}) collective-permute-start(bf16[18,1152]{1,0:T(8,128)(2,1)S(1)} %pad_maximum_fusion.refs_0_), channel_id=1, source_target_pairs={{0,4},{2,6},{4,0},{6,2},{1,5},{3,7},{5,1},{7,3},{8,12},{10,14},{12... | collective-permute-start | bytes 124424 | tf_op jit(solution)/shard_map/ppermute | solution.py:21
  8.2 4.2 %collective-permute-start.1 = (bf16[18,1152]{1,0:T(8,128)(2,1)S(1)}, bf16[18,1152]{1,0:T(8,128)(2,1)S(1)}, u32[]{:S(2)}, u32[]{:S(2)}) collective-permute-start(bf16[18,1152]{1,0:T(8,128)(2,1)S(1)} %pad_maximum_fusion.refs_0_), channel_id=1, source_target_pairs={{0,6},{2,0},{4,2},{6,4},{1,7},{3,1},{5,3},{7,5},{8,14},{10,8},{12,... | collective-permute-start | bytes 124424 | tf_op jit(solution)/shard_map/ppermute | solution.py:21
  14.9 20.6 %collective-permute-start.9 = (bf16[128,1280]{1,0:T(8,128)(2,1)S(1)}, bf16[128,1280]{1,0:T(8,128)(2,1)S(1)}, u32[]{:S(2)}, u32[]{:S(2)}) collective-permute-start(bf16[128,1280]{1,0:T(8,128)(2,1)S(1)} %fusion.1.refs_8_), channel_id=1, source_target_pairs={{0,2},{2,4},{4,6},{6,0},{1,3},{3,5},{5,7},{7,1},{8,10},{10,12},{12... | collective-permute-start | bytes 983048 | tf_op jit(solution)/shard_map/ppermute | solution.py:21
  16.5 19.1 %collective-permute-start.8 = (bf16[128,1280]{1,0:T(8,128)(2,1)S(1)}, bf16[128,1280]{1,0:T(8,128)(2,1)S(1)}, u32[]{:S(2)}, u32[]{:S(2)}) collective-permute-start(bf16[128,1280]{1,0:T(8,128)(2,1)S(1)} %fusion.1.refs_8_), channel_id=1, source_target_pairs={{0,4},{2,6},{4,0},{6,2},{1,5},{3,7},{5,1},{7,3},{8,12},{10,14},{12... | collective-permute-start | bytes 983048 | tf_op jit(solution)/shard_map/ppermute | solution.py:21
  19.4 16.2 %collective-permute-start.7 = (bf16[128,1280]{1,0:T(8,128)(2,1)S(1)}, bf16[128,1280]{1,0:T(8,128)(2,1)S(1)}, u32[]{:S(2)}, u32[]{:S(2)}) collective-permute-start(bf16[128,1280]{1,0:T(8,128)(2,1)S(1)} %fusion.1.refs_8_), channel_id=1, source_target_pairs={{0,6},{2,0},{4,2},{6,4},{1,7},{3,1},{5,3},{7,5},{8,14},{10,8},{12,... | collective-permute-start | bytes 983048 | tf_op jit(solution)/shard_map/ppermute | solution.py:21
  20.8 14.8 %collective-permute-start.6 = (bf16[128,1152]{1,0:T(8,128)(2,1)S(1)}, bf16[128,1152]{1,0:T(8,128)(2,1)S(1)}, u32[]{:S(2)}, u32[]{:S(2)}) collective-permute-start(bf16[128,1152]{1,0:T(8,128)(2,1)S(1)} %collective-permute-done.4.refs_9_), channel_id=1, source_target_pairs={{0,8},{1,9},{2,10},{3,11},{4,12},{5,13},{6,14},{7,15},{8,16},{9,17... | collective-permute-start | bytes 884744 | tf_op jit(solution)/shard_map/ppermute | solution.py:25
  20.8 10.9 %collective-permute-start.5 = (bf16[72,1152]{1,0:T(8,128)(2,1)S(1)}, bf16[72,1152]{1,0:T(8,128)(2,1)S(1)}, u32[]{:S(2)}, u32[]{:S(2)}) collective-permute-start(bf16[72,1152]{1,0:T(8,128)(2,1)S(1)} %shard_map.59), channel_id=1, source_target_pairs={{0,232},{1,224},{2,248},{3,208},{4,192},{5,200},{6,240},{7,216},{8... | collective-permute-start | bytes 497672 | tf_op jit(solution)/shard_map/ppermute | solution.py:109
  35.6 11.4 %collective-permute-start.10 = (bf16[128,1152]{1,0:T(8,128)(2,1)S(1)}, bf16[128,1152]{1,0:T(8,128)(2,1)S(1)}, u32[]{:S(2)}, u32[]{:S(2)}) collective-permute-start(bf16[128,1152]{1,0:T(8,128)(2,1)S(1)} %collective-permute-done.6.refs_10_), channel_id=1, source_target_pairs={{0,8},{1,9},{2,10},{3,11},{4,12},{5,13},{6,14},{7,15},{8,16},{9,17... | collective-permute-start | bytes 884744 | tf_op jit(solution)/shard_map/ppermute | solution.py:25
  35.7 6.6 %collective-permute-start.13 = (bf16[72,1152]{1,0:T(8,128)(2,1)S(1)}, bf16[72,1152]{1,0:T(8,128)(2,1)S(1)}, u32[]{:S(2)}, u32[]{:S(2)}) collective-permute-start(bf16[72,1152]{1,0:T(8,128)(2,1)S(1)} %collective-permute-done.5.refs_0_), channel_id=1, source_target_pairs={{6,0},{193,1},{0,2},{195,3},{2,4},{197,5},{4,6},{199,7},{14,8},{20... | collective-permute-start | bytes 497672 | tf_op jit(solution)/shard_map/ppermute | solution.py:44
  35.8 8.7 %collective-permute-start.12 = (bf16[72,1152]{1,0:T(8,128)(2,1)S(1)}, bf16[72,1152]{1,0:T(8,128)(2,1)S(1)}, u32[]{:S(2)}, u32[]{:S(2)}) collective-permute-start(bf16[72,1152]{1,0:T(8,128)(2,1)S(1)} %collective-permute-done.5.refs_0_), channel_id=1, source_target_pairs={{4,0},{129,1},{6,2},{131,3},{0,4},{133,5},{2,6},{135,7},{12,8},{13... | collective-permute-start | bytes 497672 | tf_op jit(solution)/shard_map/ppermute | solution.py:44
  39.4 5.6 %collective-permute-start.11 = (bf16[72,1152]{1,0:T(8,128)(2,1)S(1)}, bf16[72,1152]{1,0:T(8,128)(2,1)S(1)}, u32[]{:S(2)}, u32[]{:S(2)}) collective-permute-start(bf16[72,1152]{1,0:T(8,128)(2,1)S(1)} %collective-permute-done.5.refs_0_), channel_id=1, source_target_pairs={{2,0},{65,1},{4,2},{67,3},{6,4},{69,5},{0,6},{71,7},{10,8},{73,9},... | collective-permute-start | bytes 497672 | tf_op jit(solution)/shard_map/ppermute | solution.py:44
  47.7 19.6 %collective-permute-start.18 = (bf16[288,1152]{1,0:T(8,128)(2,1)S(1)}, bf16[288,1152]{1,0:T(8,128)(2,1)S(1)}, u32[]{:S(2)}, u32[]{:S(2)}) collective-permute-start(bf16[288,1152]{1,0:T(8,128)(2,1)S(1)} %shard_map.60.refs_0_), channel_id=1, source_target_pairs={{192,0},{7,1},{194,2},{1,3},{196,4},{3,5},{198,6},{5,7},{200,8},{1... | collective-permute-start | bytes 1990664 | tf_op jit(solution)/shard_map/ppermute | solution.py:44
  49.0 24.3 %collective-permute-start.17 = (bf16[288,1152]{1,0:T(8,128)(2,1)S(1)}, bf16[288,1152]{1,0:T(8,128)(2,1)S(1)}, u32[]{:S(2)}, u32[]{:S(2)}) collective-permute-start(bf16[288,1152]{1,0:T(8,128)(2,1)S(1)} %shard_map.60.refs_0_), channel_id=1, source_target_pairs={{128,0},{5,1},{130,2},{7,3},{132,4},{1,5},{134,6},{3,7},{136,8},{1... | collective-permute-start | bytes 1990664 | tf_op jit(solution)/shard_map/ppermute | solution.py:44
  50.2 23.2 %collective-permute-start.16 = (bf16[288,1152]{1,0:T(8,128)(2,1)S(1)}, bf16[288,1152]{1,0:T(8,128)(2,1)S(1)}, u32[]{:S(2)}, u32[]{:S(2)}) collective-permute-start(bf16[288,1152]{1,0:T(8,128)(2,1)S(1)} %shard_map.60.refs_0_), channel_id=1, source_target_pairs={{64,0},{3,1},{66,2},{5,3},{68,4},{7,5},{70,6},{1,7},{72,8},{11,9},... | collective-permute-start | bytes 1990664 | tf_op jit(solution)/shard_map/ppermute | solution.py:44
  51.7 21.6 %collective-permute-start.15 = (bf16[288,1152]{1,0:T(8,128)(2,1)S(1)}, bf16[288,1152]{1,0:T(8,128)(2,1)S(1)}, u32[]{:S(2)}, u32[]{:S(2)}) collective-permute-start(bf16[288,1152]{1,0:T(8,128)(2,1)S(1)} %shard_map.60.refs_0_), channel_id=1, source_target_pairs={{0,1},{1,0},{2,3},{3,2},{4,5},{5,4},{6,7},{7,6},{8,9},{9,8},{10,11... | collective-permute-start | bytes 1990664 | tf_op jit(solution)/shard_map/ppermute | solution.py:21
  53.8 13.5 %collective-permute-start.14 = (bf16[128,1152]{1,0:T(8,128)(2,1)}, bf16[128,1152]{1,0:T(8,128)(2,1)S(1)}, u32[]{:S(2)}, u32[]{:S(2)}) collective-permute-start(bf16[128,1152]{1,0:T(8,128)(2,1)} %copy-done.20), channel_id=1, source_target_pairs={{0,8},{1,9},{2,10},{3,11},{4,12},{5,13},{6,14},{7,15},{8,16},{9,17... | collective-permute-start | bytes 884744 | tf_op jit(solution)/shard_map/ppermute | solution.py:25
  73.5 3.2 %collective-permute-start.20 = (bf16[288,1152]{1,0:T(8,128)(2,1)S(1)}, bf16[288,1152]{1,0:T(8,128)(2,1)}, u32[]{:S(2)}, u32[]{:S(2)}) collective-permute-start(bf16[288,1152]{1,0:T(8,128)(2,1)S(1)} %collective-permute-done.17.refs_2_), channel_id=1, source_target_pairs={{0,1},{1,0},{2,3},{3,2},{4,5},{5,4},{6,7},{7,6},{8,9},{9,8},{10,11... | collective-permute-start | bytes 1990664 | tf_op jit(solution)/shard_map/ppermute | solution.py:21
  74.0 3.6 %collective-permute-start.21 = (bf16[288,1152]{1,0:T(8,128)(2,1)S(1)}, bf16[288,1152]{1,0:T(8,128)(2,1)}, u32[]{:S(2)}, u32[]{:S(2)}) collective-permute-start(bf16[288,1152]{1,0:T(8,128)(2,1)S(1)} %collective-permute-done.18.refs_3_), channel_id=1, source_target_pairs={{0,1},{1,0},{2,3},{3,2},{4,5},{5,4},{6,7},{7,6},{8,9},{9,8},{10,11... | collective-permute-start | bytes 1990664 | tf_op jit(solution)/shard_map/ppermute | solution.py:21
  83.8 7.1 %collective-permute-start.22 = (bf16[512,1280]{1,0:T(8,128)(2,1)}, bf16[512,1280]{1,0:T(8,128)(2,1)S(1)}, u32[]{:S(2)}, u32[]{:S(2)}) collective-permute-start(bf16[512,1280]{1,0:T(8,128)(2,1)} %get-tuple-element.66.own_emb), channel_id=1, source_target_pairs={{0,1},{1,0},{2,3},{3,2},{4,5},{5,4},{6,7},{7,6},{8,9},{9,8},{10,11... | collective-permute-start | bytes 3932168 | tf_op jit(solution)/shard_map/ppermute | solution.py:21
  94.7 9.4 %collective-permute-start.24 = (bf16[128,1152]{1,0:T(8,128)(2,1)S(1)}, bf16[128,1152]{1,0:T(8,128)(2,1)S(1)}, u32[]{:S(2)}, u32[]{:S(2)}) collective-permute-start(bf16[128,1152]{1,0:T(8,128)(2,1)S(1)} %get-tuple-element.76), channel_id=1, source_target_pairs={{0,248},{1,249},{2,250},{3,251},{4,252},{5,253},{6,254},{7,255},{8... | collective-permute-start | bytes 884744 | tf_op jit(solution)/shard_map/ppermute | solution.py:25
  94.8 22.0 %collective-permute-start.33 = (bf16[128,1152]{1,0:T(8,128)(2,1)S(1)}, bf16[128,1152]{1,0:T(8,128)(2,1)S(1)}, u32[]{:S(2)}, u32[]{:S(2)}) collective-permute-start(bf16[128,1152]{1,0:T(8,128)(2,1)S(1)} %get-tuple-element.93), channel_id=1, source_target_pairs={{0,24},{8,32},{16,40},{24,48},{32,56},{40,0},{48,8},{56,16},{1,25}... | collective-permute-start | bytes 884744 | tf_op jit(solution)/shard_map/ppermute | solution.py:21
  100.7 21.7 %collective-permute-start.23 = (bf16[128,1152]{1,0:T(8,128)(2,1)S(1)}, bf16[128,1152]{1,0:T(8,128)(2,1)S(1)}, u32[]{:S(2)}, u32[]{:S(2)}) collective-permute-start(bf16[128,1152]{1,0:T(8,128)(2,1)S(1)} %get-tuple-element.72), channel_id=1, source_target_pairs={{0,1},{1,0},{2,3},{3,2},{4,5},{5,4},{6,7},{7,6},{8,9},{9,8},{10,11... | collective-permute-start | bytes 884744 | tf_op jit(solution)/shard_map/ppermute | solution.py:21
  101.3 6.5 %collective-permute-start.29 = (bf16[128,1152]{1,0:T(8,128)(2,1)S(1)}, bf16[128,1152]{1,0:T(8,128)(2,1)S(1)}, u32[]{:S(2)}, u32[]{:S(2)}) collective-permute-start(bf16[128,1152]{1,0:T(8,128)(2,1)S(1)} %get-tuple-element.84), channel_id=1, source_target_pairs={{0,1},{1,0},{2,3},{3,2},{4,5},{5,4},{6,7},{7,6},{8,9},{9,8},{10,11... | collective-permute-start | bytes 884744 | tf_op jit(solution)/shard_map/ppermute | solution.py:21
  104.0 4.9 %collective-permute-start.31 = (bf16[128,1152]{1,0:T(8,128)(2,1)S(1)}, bf16[128,1152]{1,0:T(8,128)(2,1)S(1)}, u32[]{:S(2)}, u32[]{:S(2)}) collective-permute-start(bf16[128,1152]{1,0:T(8,128)(2,1)S(1)} %get-tuple-element.87), channel_id=1, source_target_pairs={{0,1},{1,0},{2,3},{3,2},{4,5},{5,4},{6,7},{7,6},{8,9},{9,8},{10,11... | collective-permute-start | bytes 884744 | tf_op jit(solution)/shard_map/ppermute | solution.py:21
  104.1 15.4 %collective-permute-start.25 = (bf16[128,1152]{1,0:T(8,128)(2,1)S(1)}, bf16[128,1152]{1,0:T(8,128)(2,1)S(1)}, u32[]{:S(2)}, u32[]{:S(2)}) collective-permute-start(bf16[128,1152]{1,0:T(8,128)(2,1)S(1)} %add_convert_fusion.4), channel_id=1, source_target_pairs={{0,248},{1,249},{2,250},{3,251},{4,252},{5,253},{6,254},{7,255},{8... | collective-permute-start | bytes 884744 | tf_op jit(solution)/shard_map/ppermute | solution.py:25
  107.9 14.4 %collective-permute-start.27 = (bf16[128,1152]{1,0:T(8,128)(2,1)S(1)}, bf16[128,1152]{1,0:T(8,128)(2,1)S(1)}, u32[]{:S(2)}, u32[]{:S(2)}) collective-permute-start(bf16[128,1152]{1,0:T(8,128)(2,1)S(1)} %add_convert_fusion.3), channel_id=1, source_target_pairs={{0,2},{2,4},{4,6},{6,0},{1,3},{3,5},{5,7},{7,1},{8,10},{10,12},{12... | collective-permute-start | bytes 884744 | tf_op jit(solution)/shard_map/ppermute | solution.py:21
  109.0 17.1 %collective-permute-start.30 = (bf16[128,1152]{1,0:T(8,128)(2,1)S(1)}, bf16[128,1152]{1,0:T(8,128)(2,1)S(1)}, u32[]{:S(2)}, u32[]{:S(2)}) collective-permute-start(bf16[128,1152]{1,0:T(8,128)(2,1)S(1)} %add_convert_fusion.1), channel_id=1, source_target_pairs={{0,4},{2,6},{4,0},{6,2},{1,5},{3,7},{5,1},{7,3},{8,12},{10,14},{12... | collective-permute-start | bytes 884744 | tf_op jit(solution)/shard_map/ppermute | solution.py:21
  116.8 16.6 %collective-permute-start.32 = (bf16[128,1152]{1,0:T(8,128)(2,1)S(1)}, bf16[128,1152]{1,0:T(8,128)(2,1)S(1)}, u32[]{:S(2)}, u32[]{:S(2)}) collective-permute-start(bf16[128,1152]{1,0:T(8,128)(2,1)S(1)} %add_convert_fusion), channel_id=1, source_target_pairs={{0,6},{2,0},{4,2},{6,4},{1,7},{3,1},{5,3},{7,5},{8,14},{10,8},{12,... | collective-permute-start | bytes 884744 | tf_op jit(solution)/shard_map/ppermute | solution.py:21
  119.5 12.0 %collective-permute-start.34 = (bf16[128,1152]{1,0:T(8,128)(2,1)S(1)}, bf16[128,1152]{1,0:T(8,128)(2,1)S(1)}, u32[]{:S(2)}, u32[]{:S(2)}) collective-permute-start(bf16[128,1152]{1,0:T(8,128)(2,1)S(1)} %collective-permute-done.33), channel_id=1, source_target_pairs={{0,8},{1,9},{2,10},{3,11},{4,12},{5,13},{6,14},{7,15},{8,16},{9,17... | collective-permute-start | bytes 884744 | tf_op jit(solution)/shard_map/ppermute | solution.py:271
  122.3 9.2 %collective-permute-start.28 = (bf16[128,1152]{1,0:T(8,128)(2,1)S(1)}, bf16[128,1152]{1,0:T(8,128)(2,1)S(1)}, u32[]{:S(2)}, u32[]{:S(2)}) collective-permute-start(bf16[128,1152]{1,0:T(8,128)(2,1)S(1)} %add_convert_fusion.2), channel_id=1, source_target_pairs={{0,248},{1,249},{2,250},{3,251},{4,252},{5,253},{6,254},{7,255},{8... | collective-permute-start | bytes 884744 | tf_op jit(solution)/shard_map/ppermute | solution.py:25
  (25 other events, 228.0 us)
